TPU v7x, 256 devices: a whole 4x4x8 slice. The times are simulated.
256 devices in a mesh: row: 16 (over y, x), col: 16 (over z, core).
Axes of the slice: x: 4, y: 4, z: 8, core: 2. Of those that a mesh axis runs over, the one named last changes fastest.
Arguments:
- matrix: bfloat16 [24576, 24576], P('row', 'col'), may hold values from -6 to 6
- inverses: bfloat16 [2, 256, 256], replicated, may hold values from -0.09 to 0.1, as said below
Outputs:
- factored: bfloat16 [24576, 24576], P('row', 'col')
- panels: bfloat16 [24576, 512], P('row')
Inputs may be any that keep to these rules, and one draw needn't show every extreme that they name: `inverses`: each of the two matrices is lower triangular with a diagonal between 0.05 and 0.1.
All inputs are finite; a program needn't handle non-finite values.
Results may differ from a plain program's by a relative error of at most 0.0057.
Values may be sent and summed in bfloat16 or wider, within the bound.
No kernel may reach another device: no remote copies, remote signals or barrier semaphores. Data moves between devices by JAX's collectives and lax.ppermute only.
A program may use at most 128 MiB of HBM per device.

v0:
```python
import jax
import jax.numpy as jnp
from jax import lax
from jax.sharding import PartitionSpec as P


def from_root(value, axis, source):
    kept = jnp.where(lax.axis_index(axis) == source, value, 0).astype(value.dtype)
    return lax.psum(kept, axis)


def outer_term(left_rows, right_rows):
    return lax.dot_general(
        left_rows, right_rows, (((1,), (1,)), ((), ())), preferred_element_type=jnp.float32
    )


def shards(matrix, inverses):
    width = inverses.shape[1]
    rows_local = matrix.shape[0]
    row_count = lax.axis_size("row")
    col_count = lax.axis_size("col")
    row_rank = lax.axis_index("row")
    col_rank = lax.axis_index("col")
    blocks_row = rows_local // width
    blocks_col = matrix.shape[1] // width
    ratio_blocks = col_count // row_count
    global_rows = jnp.repeat(jnp.arange(blocks_row, dtype=jnp.int32) * row_count + row_rank, width)
    source_row = col_rank % row_count
    source_slot = col_rank // row_count

    def factor(panel, inverse, start_block, owner_col):
        product = jnp.dot(panel, inverse.T, preferred_element_type=jnp.float32)
        masked = jnp.where((global_rows >= start_block)[:, None], product, 0.0).astype(jnp.bfloat16)
        return from_root(masked, "col", owner_col)

    def columns_of(left_rows):
        gathered = lax.all_gather(left_rows, "row", axis=0, tiled=True)
        gathered = gathered.reshape(row_count, blocks_col, ratio_blocks, width, width)
        mine = lax.dynamic_index_in_dim(gathered, source_row, 0, keepdims=False)
        mine = lax.dynamic_index_in_dim(mine, source_slot, 1, keepdims=False)
        return mine.reshape(blocks_col * width, width)

    first_rows = factor(matrix[:, :width], inverses[0], 1, 0)
    first_cols = columns_of(first_rows)
    partial_value = matrix.astype(jnp.float32) - outer_term(first_rows, first_cols)
    head = partial_value[:, :width].astype(jnp.bfloat16)
    second_rows = factor(head, inverses[1], 2, 1)
    second_cols = columns_of(second_rows)
    factored = (partial_value - outer_term(second_rows, second_cols)).astype(jnp.bfloat16)
    return (factored, jnp.concatenate([first_rows, second_rows], axis=1))


def solution(mesh):
    return jax.shard_map(
        shards,
        mesh=mesh,
        in_specs=(P("row", "col"), P()),
        out_specs=(P("row", "col"), P("row", None)),
        check_vma=False,
    )
```

profile of v0, /device:TPU:99, one launch (start us, length us, event | category | flops | bytes accessed | tf_op | source)
XLA Modules:
  0.0 454.7 jit_solution(4977230878266750554)
XLA Ops:
  7.2 0.0 all-reduce.3.cloned.1.call-start
  7.2 0.1 broadcast_in_dim.30
  7.3 2.5 fusion.4
  9.8 0.0 all-reduce.3.cloned.1.call-update
  9.8 0.0 all-gather.3.cloned.1.call-start
  9.8 113.6 %all-reduce.3.cloned.1.call-done = bf16[1536,256]{1,0:T(8,128)(2,1)} async-done(((bf16[1536,256]{1,0:T(8,128)(2,1)}), bf16[1536,256]{1,0:T(8,128)(2,1)}) %all-reduce.3.cloned.1.call-update) | async-done | bytes 786448 | tf_op jit(solution)/shard_map/psum | solution.py:9
  123.4 0.0 all-gather.3.cloned.1.call-update
  123.5 0.0 all-reduce.5.cloned.1.call-start
  123.5 0.1 broadcast_in_dim.34
  123.6 97.8 %all-gather.3.cloned.1.call-done = bf16[24576,256]{1,0:T(8,128)(2,1)} async-done(((bf16[1536,256]{1,0:T(8,128)(2,1)}), bf16[24576,256]{1,0:T(8,128)(2,1)}) %all-gather.3.cloned.1.call-update) | async-done | bytes 12582928 | tf_op jit(solution)/shard_map/all_gather | solution.py:38
  221.4 1.2 constant_dynamic-slice_fusion.1
  222.6 0.0 copy-start.3
  222.6 4.0 convolution_subtract_fusion.1
  226.7 0.0 copy-start
  226.7 3.5 copy-done
  230.2 0.0 copy-done.3
  230.2 0.0 copy-start.1
  230.2 1.3 fusion.3
  231.5 0.0 all-reduce.5.cloned.1.call-update
  231.5 0.0 all-gather.5.cloned.1.call-start
  231.6 110.6 %all-reduce.5.cloned.1.call-done = bf16[1536,256]{1,0:T(8,128)(2,1)} async-done(((bf16[1536,256]{1,0:T(8,128)(2,1)}), bf16[1536,256]{1,0:T(8,128)(2,1)}) %all-reduce.5.cloned.1.call-update) | async-done | bytes 786448 | tf_op jit(solution)/shard_map/psum | solution.py:9
  342.1 0.0 copy-start.2
  342.1 0.0 all-gather.5.cloned.1.call-update
  342.2 0.0 copy-done.1
  342.2 2.5 pad_maximum_fusion
  344.6 95.0 %all-gather.5.cloned.1.call-done = bf16[24576,256]{1,0:T(8,128)(2,1)} async-done(((bf16[1536,256]{1,0:T(8,128)(2,1)}), bf16[24576,256]{1,0:T(8,128)(2,1)}) %all-gather.5.cloned.1.call-update) | async-done | bytes 12582928 | tf_op jit(solution)/shard_map/all_gather | solution.py:38
  439.7 1.2 constant_dynamic-slice_fusion
  440.8 0.0 copy-done.2
  440.9 7.3 %fusion = bf16[1536,1536]{1,0:T(8,128)(2,1)} fusion(f32[1536,1536]{1,0:T(8,128)} %copy-done, bf16[1536,256]{1,0:T(8,128)(2,1)S(1)} %copy-done.2, bf16[1536,256]{1,0:T(8,128)(2,1)S(1)} %bitcast.15), kind=kOutput, calls=%fused_computation.2 | convolution fusion | flops 1212678144 | bytes 15728640 | tf_op jit(solution)/shard_map/dot_general | solution.py:13
  (3 shorter events, 0.0 us)
Async XLA Ops:
  7.2 116.3 %all-reduce.3.cloned.1.call-start = ((), (), s32[]{:S(2)}) async-start(), calls=%async_computation | async-start | bytes 1572864 | tf_op jit(solution)/shard_map/psum | solution.py:9
  9.8 211.6 %all-gather.3.cloned.1.call-start = ((), (), s32[]{:S(2)}) async-start(), calls=%async_computation.1 | async-start | bytes 13369344 | tf_op jit(solution)/shard_map/all_gather | solution.py:38
  123.5 218.7 %all-reduce.5.cloned.1.call-start = ((), (), s32[]{:S(2)}) async-start(), calls=%async_computation.2 | async-start | bytes 1572864 | tf_op jit(solution)/shard_map/psum | solution.py:9
  222.6 7.6 %copy-start.3 = (bf16[2,256,256]{2,1,0:T(8,128)(2,1)S(1)}, bf16[2,256,256]{2,1,0:T(8,128)(2,1)}, u32[]{:S(2)}) copy-start(bf16[2,256,256]{2,1,0:T(8,128)(2,1)} %param.3) | copy-start | bytes 786436
  226.7 3.5 copy-start
  230.2 112.0 %copy-start.1 = (bf16[1536,256]{1,0:T(8,128)(2,1)S(1)}, bf16[1536,256]{1,0:T(8,128)(2,1)}, u32[]{:S(2)}) copy-start(bf16[1536,256]{1,0:T(8,128)(2,1)} %all-reduce.3.cloned.1.call-done) | copy-start | bytes 2359300
  231.5 208.1 %all-gather.5.cloned.1.call-start = ((), (), s32[]{:S(2)}) async-start(), calls=%async_computation.3 | async-start | bytes 13369344 | tf_op jit(solution)/shard_map/all_gather | solution.py:38
  342.1 98.7 %copy-start.2 = (bf16[1536,256]{1,0:T(8,128)(2,1)S(1)}, bf16[1536,256]{1,0:T(8,128)(2,1)}, u32[]{:S(2)}) copy-start(bf16[1536,256]{1,0:T(8,128)(2,1)} %all-reduce.5.cloned.1.call-done) | copy-start | bytes 2359300
Sparse Core Ops, SparseCore 0:
  10.9 112.5 all-reduce.2
  126.2 95.1 all-gather.2
  231.7 110.4 all-reduce.4
  344.4 95.1 all-gather.4
where the time goes:
time: 457 us; the launch traced here: 455 us
  waiting for transfers between devices  417 us (91%)
  matrix products  15.1 us (3%)
  between operations  13.8 us (3%)
  local copies, waits for them, and re-layouts  6.09 us (1%)
    psum x2, waiting for transfers between devices, from_root(): return lax.psum(kept, axis)  224 us
    all_gather x2, waiting for transfers between devices, columns_of(): gathered = lax.all_gather(left_rows, 'row', axis=0, tiled=True)  193 us
    dot_general x2, matrix products, outer_term(): lax.dot_general(left_rows, right_rows, (((1,), (1,)), ((), ())), preferre...  11.3 us
  transfers between devices with their start and end apart: 4, of which 4 were waited for; matrix products, arithmetic and copies ran while one was open for 1% of the time, Pallas kernels for 0%

commit v1 on v0

v1 whole, which is shorter than its diff:
```python
import functools

import jax
import jax.numpy as jnp
from jax import lax
from jax.experimental import pallas as pl
from jax.experimental.pallas import tpu as pltpu
from jax.sharding import PartitionSpec as P

BOTH = ("row", "col")
NB = 256
SLOTS = 6
LINE = 8
CUT = NB // LINE


def dot_t(left, right):
    return lax.dot_general(
        left, right, (((1,), (1,)), ((), ())), preferred_element_type=jnp.float32
    )


def finish_kernel(where_ref, matrix, inverses, own, near1, near2, near3, far,
                  swap1, swap2, swap3, swap4, cols, factored, panels,
                  held, inv, rows_x, cols_x, head_g, rows_f, cols_f, result,
                  sem_m, sem_x, sem_o):
    row, col = where_ref[0], where_ref[1]
    z, core = col // 2, lax.rem(col, 2)
    copies = []

    def start(src, dst, sem):
        copy = pltpu.make_async_copy(src, dst, sem)
        copy.start()
        return copy

    early = [start(inverses, inv, sem_x.at[0])]
    for h in range(2):
        for s in range(LINE):
            early.append(start(cols.at[2 * s + h], cols_x.at[h, :, s], sem_x.at[0]))

    def place(msg, slot):
        for h in range(2):
            copies.append(start(msg.at[pl.ds(SLOTS * h, SLOTS)], rows_x.at[h, :, slot], sem_x.at[1]))
        copies.append(start(msg.at[2 * SLOTS], head_g.at[slot], sem_x.at[1]))

    place(own, z)
    for d, (near, swap) in enumerate(((near1, swap1), (near2, swap2), (near3, swap3)), 1):
        up, down = lax.rem(z + d, LINE), lax.rem(z + LINE - d, LINE)
        place(near, jnp.where(core == 0, up, down))
        place(swap, jnp.where(core == 0, down, up))
    across = lax.rem(z + LINE // 2, LINE)
    copies.append(start(far.at[pl.ds(0, SLOTS)], rows_x.at[core, :, across], sem_x.at[1]))
    copies.append(start(swap4.at[pl.ds(0, SLOTS)], rows_x.at[1 - core, :, across], sem_x.at[1]))
    copies.append(start(far.at[SLOTS], head_g.at[across], sem_x.at[1]))
    loads = [start(matrix.at[pl.ds(NB * b, NB)], held.at[b], sem_m.at[b]) for b in range(SLOTS)]

    for c in early + copies:
        c.wait()
    lower0, lower1 = inv[0], inv[1]
    pivot = dot_t(head_g[...].reshape(NB, NB), lower0).astype(jnp.bfloat16)

    def factor(x, f, rank):
        for b in range(SLOTS):
            block = b * 16 + rank
            at = pl.ds(NB * b, NB)
            first = dot_t(x[0, b].reshape(NB, NB), lower0)
            first = jnp.where(block >= 1, first, 0.0).astype(jnp.bfloat16)
            f[at, pl.ds(0, NB)] = first
            head = (x[1, b].reshape(NB, NB).astype(jnp.float32) - dot_t(first, pivot)).astype(jnp.bfloat16)
            second = dot_t(head, lower1)
            f[at, pl.ds(NB, NB)] = jnp.where(block >= 2, second, 0.0).astype(jnp.bfloat16)

    factor(rows_x, rows_f, row)
    stores = [start(rows_f, panels, sem_o.at[SLOTS])]
    factor(cols_x, cols_f, col)
    for b in range(SLOTS):
        loads[b].wait()
        at = pl.ds(NB * b, NB)
        value = held[b].astype(jnp.float32) - dot_t(rows_f[at, :], cols_f[...])
        result[b] = value.astype(jnp.bfloat16)
        stores.append(start(result.at[b], factored.at[at], sem_o.at[b]))
    for c in stores:
        c.wait()


def finish(place, matrix, inverses, *pieces):
    any_space = pl.BlockSpec(memory_space=pl.ANY)
    rows, columns = matrix.shape
    return pl.pallas_call(
        finish_kernel,
        out_shape=(
            jax.ShapeDtypeStruct(matrix.shape, jnp.bfloat16),
            jax.ShapeDtypeStruct((rows, 2 * NB), jnp.bfloat16),
        ),
        in_specs=[pl.BlockSpec(memory_space=pltpu.SMEM)] + [any_space] * (2 + len(pieces)),
        out_specs=(any_space, any_space),
        scratch_shapes=[
            pltpu.VMEM((SLOTS, NB, columns), jnp.bfloat16),
            pltpu.VMEM((2, NB, NB), jnp.bfloat16),
            pltpu.VMEM((2, SLOTS, LINE, CUT, NB), jnp.bfloat16),
            pltpu.VMEM((2, SLOTS, LINE, CUT, NB), jnp.bfloat16),
            pltpu.VMEM((LINE, CUT, NB), jnp.bfloat16),
            pltpu.VMEM((rows, 2 * NB), jnp.bfloat16),
            pltpu.VMEM((columns, 2 * NB), jnp.bfloat16),
            pltpu.VMEM((SLOTS, NB, columns), jnp.bfloat16),
            pltpu.SemaphoreType.DMA((SLOTS,)),
            pltpu.SemaphoreType.DMA((2,)),
            pltpu.SemaphoreType.DMA((SLOTS + 1,)),
        ],
        compiler_params=pltpu.CompilerParams(vmem_limit_bytes=40 * 1024 * 1024),
        cost_estimate=pl.CostEstimate(
            flops=2 * rows * columns * 2 * NB, bytes_accessed=4 * rows * columns, transcendentals=0
        ),
    )(place, matrix, inverses, *pieces)


def moves(step):
    pairs = []
    for row in range(16):
        for z in range(LINE):
            for core in range(2):
                to = step(row, z, core)
                if to is not None:
                    pairs.append((row * 16 + 2 * z + core, to[0] * 16 + 2 * (to[1] % LINE) + to[2]))
    return pairs


def send(value, pairs):
    return lax.ppermute(value, BOTH, pairs)


def shards(matrix, inverses):
    row, col = lax.axis_index("row"), lax.axis_index("col")
    z, core = col // 2, col % 2
    cut = matrix[:, :NB].reshape(SLOTS, LINE, CUT, NB)
    mine = jnp.where(z == 0, cut[:, 0], 0)
    for d in (1, 2, 3, 7, 6, 5, 4):
        mine = mine + send(cut[:, d], moves(lambda r, zz, h: (r, d, h) if zz == 0 else None))
    crossed = send(mine, [(r * 16 + c, c * 16 + r) for r in range(16) for c in range(16)])
    pivot = lax.all_to_all(jnp.broadcast_to(mine[:1], (16, CUT, NB)), "row", 0, 0, tiled=True)[1:2]
    theirs = send(jnp.concatenate([mine, pivot]), moves(lambda r, zz, h: (r, zz, 1 - h)))
    is0 = core == 0
    own = jnp.concatenate([
        jnp.where(is0, mine, theirs[:SLOTS]),
        jnp.where(is0, theirs[:SLOTS], mine),
        jnp.where(is0, pivot, theirs[SLOTS:]),
    ])
    near = [send(own, moves(lambda r, zz, h: (r, zz - d if h == 0 else zz + d, h))) for d in (1, 2, 3)]
    far = send(jnp.concatenate([mine, own[2 * SLOTS:]]), moves(lambda r, zz, h: (r, zz + 4, h)))
    cols = lax.all_to_all(jnp.broadcast_to(crossed[None], (16,) + crossed.shape), "row", 0, 0, tiled=True)
    swaps = [send(v, moves(lambda r, zz, h: (r, zz, 1 - h))) for v in (*near, far)]
    place = jnp.stack([row, col]).astype(jnp.int32)
    return finish(place, matrix, inverses, own, *near, far, *swaps, cols)


def solution(mesh):
    return jax.shard_map(
        shards,
        mesh=mesh,
        in_specs=(P("row", "col"), P()),
        out_specs=(P("row", "col"), P("row", None)),
        check_vma=False,
    )
```

time: 457 us -> 94.5 us (0.21)
  waiting for transfers between devices: 417 us -> 18.4 us
  starting transfers between devices: 0.16 us -> 58.5 us
  matrix products: 15.1 us -> 0 us
  between operations: 13.8 us -> 1 us
  Pallas kernels: 0 us -> 9.14 us
    psum x2 -> x0, waiting for transfers between devices: 224 us -> none  [from_root(): return lax.psum(kept, axis)]
    all_gather x2 -> x0, waiting for transfers between devices: 193 us -> none  [columns_of(): gathered = lax.all_gather(left_rows, 'row', axis=0, tiled=True)]
    ppermute x0 -> x17, starting transfers between devices: none -> 37.5 us  [send(): return lax.ppermute(value, BOTH, pairs)]
    all_to_all x0 -> x2, starting transfers between devices: none -> 21 us  [the longest x1 14.1 us: shards(): lax.all_to_all(jnp.broadcast_to(crossed[None], (16,) + crossed.shape), 'r...]
    ppermute x0 -> x17, waiting for transfers between devices: none -> 18.4 us  [send(): return lax.ppermute(value, BOTH, pairs)]
    dot_general x4 -> x0, matrix products: 15.1 us -> none  [the longest x2 11.3 us: outer_term(): lax.dot_general(left_rows, right_rows, (((1,), (1,)), ((), ())), preferre...]
    pallas_call x0 -> x1, Pallas kernels: none -> 9.14 us  [finish(): pl.pallas_call(finish_kernel, out_shape=(jax.ShapeDtypeStruct(matrix.shap...]
  transfers between devices with their start and end apart: 4 -> 19, of which waited for: 4 -> 6; matrix products, arithmetic and copies ran while one was open for 1% -> 1% of each run, Pallas kernels for 0% -> 0%
where the time goes in v1:
time: 94.5 us; the launch traced here: 94 us
  starting transfers between devices  58.5 us (62%)
  waiting for transfers between devices  18.4 us (19%)
  Pallas kernels  9.14 us (10%)
  local copies, waits for them, and re-layouts  6.25 us (7%)
  between operations  1 us (1%)
    ppermute x17, starting transfers between devices, send(): return lax.ppermute(value, BOTH, pairs)  37.5 us
    ppermute x17, waiting for transfers between devices, send(): return lax.ppermute(value, BOTH, pairs)  18.4 us
    all_to_all x1, starting transfers between devices, shards(): lax.all_to_all(jnp.broadcast_to(crossed[None], (16,) + crossed.shape), 'r...  14.1 us
    pallas_call x1, Pallas kernels, finish(): pl.pallas_call(finish_kernel, out_shape=(jax.ShapeDtypeStruct(matrix.shap...  9.14 us
    all_to_all x1, starting transfers between devices, shards(): lax.all_to_all(jnp.broadcast_to(mine[:1], (16, CUT, NB)), 'row', 0, 0, ti...  6.92 us
    unnamed x6, local copies, waits for them, and re-layouts  2.94 us
  transfers between devices with their start and end apart: 19, of which 6 were waited for; matrix products, arithmetic and copies ran while one was open for 1% of the time, Pallas kernels for 0%

profile of v1, /device:TPU:99, one launch (start us, length us, event | category | flops | bytes accessed | tf_op | source)
XLA Modules:
  0.0 94.0 jit_solution(8532805056376843634)
XLA Ops:
  0.6 1.2 %slice.40 = bf16[1536,256]{1,0:T(8,128)(2,1)S(1)} slice(bf16[1536,1536]{1,0:T(8,128)(2,1)} %matrix.1), slice={[0:1536], [0:256]} | slice | bytes 1572864 | tf_op jit(solution)/shard_map/slice | solution.py:135
  1.8 0.1 slice_bitcast_fusion.6
  1.9 0.7 collective-permute-start
  2.6 0.7 collective-permute-start.5
  3.2 0.7 collective-permute-start.4
  3.9 0.7 collective-permute-start.3
  4.6 1.3 %collective-permute-start.2 = (bf16[6,32,256]{2,1,0:T(8,128)(2,1)S(1)}, bf16[6,32,256]{2,1,0:T(8,128)(2,1)S(1)}, u32[]{:S(2)}, u32[]{:S(2)}) collective-permute-start(bf16[6,32,256]{2,1,0:T(8,128)(2,1)S(1)} %get-tuple-element.6), channel_id=1, source_target_pairs={{0,6},{1,7},{16,22},{17,23},{32,38},{33,39},{48,54},{49,55},{64,70... | collective-permute-start | bytes 294920 | tf_op jit(solution)/shard_map/ppermute | solution.py:129
  5.9 0.0 collective-permute-done
  5.9 0.7 collective-permute-start.1
  6.6 0.0 collective-permute-done.5
  6.6 0.7 collective-permute-start.6
  7.3 0.0 collective-permute-done.4
  7.3 0.0 collective-permute-done.3
  7.3 8.5 %collective-permute-done.2 = bf16[6,32,256]{2,1,0:T(8,128)(2,1)S(1)} collective-permute-done((bf16[6,32,256]{2,1,0:T(8,128)(2,1)S(1)}, bf16[6,32,256]{2,1,0:T(8,128)(2,1)S(1)}, u32[]{:S(2)}, u32[]{:S(2)}) %collective-permute-start.2) | collective-permute-done | bytes 98336 | tf_op jit(solution)/shard_map/ppermute | solution.py:129
  15.7 0.0 collective-permute-done.1
  15.7 0.0 collective-permute-done.6
  15.8 0.7 broadcast_in_dim.19
  16.5 6.9 %all-to-all-start = ((bf16[16,32,256]{2,1,0:T(8,128)(2,1)}), bf16[16,32,256]{2,1,0:T(8,128)(2,1)S(1)}, u32[]{:S(2)}, u32[]{:S(2)}) async-start(bf16[16,32,256]{2,1,0:T(8,128)(2,1)} %broadcast_in_dim.19), calls=%async_computation | async-start | bytes 524288 | tf_op jit(solution)/shard_map/all_to_all | solution.py:140
  23.5 8.3 %collective-permute-start.16 = (bf16[6,32,256]{2,1,0:T(8,128)(2,1)S(1)}, bf16[6,32,256]{2,1,0:T(8,128)(2,1)S(1)}, u32[]{:S(2)}, u32[]{:S(2)}) collective-permute-start(bf16[6,32,256]{2,1,0:T(8,128)(2,1)S(1)} %fusion.8), channel_id=1, source_target_pairs={{0,0},{1,16},{2,32},{3,48},{4,64},{5,80},{6,96},{7,112},{8,128},{9... | collective-permute-start | bytes 294920 | tf_op jit(solution)/shard_map/ppermute | solution.py:129
  31.8 3.0 %collective-permute-done.16 = bf16[6,32,256]{2,1,0:T(8,128)(2,1)S(1)} collective-permute-done((bf16[6,32,256]{2,1,0:T(8,128)(2,1)S(1)}, bf16[6,32,256]{2,1,0:T(8,128)(2,1)S(1)}, u32[]{:S(2)}, u32[]{:S(2)}) %collective-permute-start.16) | collective-permute-done | bytes 98336 | tf_op jit(solution)/shard_map/ppermute | solution.py:129
  34.8 0.0 all-to-all-done
  34.8 1.3 %broadcast_in_dim.20 = bf16[16,6,32,256]{3,2,1,0:T(8,128)(2,1)} broadcast(bf16[6,32,256]{2,1,0:T(8,128)(2,1)S(1)} %collective-permute-done.16), dimensions={1,2,3} | broadcast | bytes 1671168 | tf_op jit(solution)/shard_map/broadcast_in_dim | solution.py:150
  36.1 0.0 copy-start.1
  36.1 14.1 %all-to-all-start.1 = ((bf16[16,6,32,256]{3,2,1,0:T(8,128)(2,1)}), bf16[16,6,32,256]{3,2,1,0:T(8,128)(2,1)S(1)}, u32[]{:S(2)}, u32[]{:S(2)}) async-start(bf16[16,6,32,256]{3,2,1,0:T(8,128)(2,1)} %broadcast_in_dim.20), calls=%async_computation.1 | async-start | bytes 3145728 | tf_op jit(solution)/shard_map/all_to_all | solution.py:150
  50.3 1.1 %collective-permute-start.7 = (bf16[7,32,256]{2,1,0:T(8,128)(2,1)S(1)}, bf16[7,32,256]{2,1,0:T(8,128)(2,1)S(1)}, u32[]{:S(2)}, u32[]{:S(2)}) collective-permute-start(bf16[7,32,256]{2,1,0:T(8,128)(2,1)S(1)} %pad_maximum_fusion.1), channel_id=1, source_target_pairs={{0,1},{1,0},{2,3},{3,2},{4,5},{5,4},{6,7},{7,6},{8,9},{9,8},{10,11... | collective-permute-start | bytes 344072 | tf_op jit(solution)/shard_map/ppermute | solution.py:129
  51.4 1.0 %collective-permute-done.7 = bf16[7,32,256]{2,1,0:T(8,128)(2,1)S(1)} collective-permute-done((bf16[7,32,256]{2,1,0:T(8,128)(2,1)S(1)}, bf16[7,32,256]{2,1,0:T(8,128)(2,1)S(1)}, u32[]{:S(2)}, u32[]{:S(2)}) %collective-permute-start.7) | collective-permute-done | bytes 114720 | tf_op jit(solution)/shard_map/ppermute | solution.py:129
  52.4 1.4 %collective-permute-start.10 = (bf16[13,32,256]{2,1,0:T(8,128)(2,1)S(1)}, bf16[13,32,256]{2,1,0:T(8,128)(2,1)S(1)}, u32[]{:S(2)}, u32[]{:S(2)}) collective-permute-start(bf16[13,32,256]{2,1,0:T(8,128)(2,1)S(1)} %pad_maximum_fusion.own), channel_id=1, source_target_pairs={{0,10},{1,7},{2,12},{3,9},{4,14},{5,11},{6,0},{7,13},{8,2},{9,15},... | collective-permute-start | bytes 638984 | tf_op jit(solution)/shard_map/ppermute | solution.py:129
  53.8 5.6 %collective-permute-start.9 = (bf16[13,32,256]{2,1,0:T(8,128)(2,1)S(1)}, bf16[13,32,256]{2,1,0:T(8,128)(2,1)S(1)}, u32[]{:S(2)}, u32[]{:S(2)}) collective-permute-start(bf16[13,32,256]{2,1,0:T(8,128)(2,1)S(1)} %pad_maximum_fusion.own), channel_id=1, source_target_pairs={{0,12},{1,5},{2,14},{3,7},{4,0},{5,9},{6,2},{7,11},{8,4},{9,13},{1... | collective-permute-start | bytes 638984 | tf_op jit(solution)/shard_map/ppermute | solution.py:129
  59.4 0.0 collective-permute-start.8
  59.4 4.3 %collective-permute-start.11 = (bf16[7,32,256]{2,1,0:T(8,128)(2,1)S(1)}, bf16[7,32,256]{2,1,0:T(8,128)(2,1)S(1)}, u32[]{:S(2)}, u32[]{:S(2)}) collective-permute-start(bf16[7,32,256]{2,1,0:T(8,128)(2,1)S(1)} %pad_maximum_fusion.2), channel_id=1, source_target_pairs={{0,8},{1,9},{2,10},{3,11},{4,12},{5,13},{6,14},{7,15},{8,0},{9,1},... | collective-permute-start | bytes 344072 | tf_op jit(solution)/shard_map/ppermute | solution.py:129
  63.7 0.0 collective-permute-done.10.near3
  63.7 1.8 %collective-permute-start.14 = (bf16[13,32,256]{2,1,0:T(8,128)(2,1)S(1)}, bf16[13,32,256]{2,1,0:T(8,128)(2,1)S(1)}, u32[]{:S(2)}, u32[]{:S(2)}) collective-permute-start(bf16[13,32,256]{2,1,0:T(8,128)(2,1)S(1)} %collective-permute-done.10.near3), channel_id=1, source_target_pairs={{0,1},{1,0},{2,3},{3,2},{4,5},{5,4},{6,7},{7,6},{8,9},{9,8},{10,11... | collective-permute-start | bytes 638984 | tf_op jit(solution)/shard_map/ppermute | solution.py:129
  65.6 5.3 %collective-permute-done.9.near2 = bf16[13,32,256]{2,1,0:T(8,128)(2,1)S(1)} collective-permute-done((bf16[13,32,256]{2,1,0:T(8,128)(2,1)S(1)}, bf16[13,32,256]{2,1,0:T(8,128)(2,1)S(1)}, u32[]{:S(2)}, u32[]{:S(2)}) %collective-permute-start.9) | collective-permute-done | bytes 213024 | tf_op jit(solution)/shard_map/ppermute | solution.py:129
  70.8 1.9 %collective-permute-start.13 = (bf16[13,32,256]{2,1,0:T(8,128)(2,1)S(1)}, bf16[13,32,256]{2,1,0:T(8,128)(2,1)S(1)}, u32[]{:S(2)}, u32[]{:S(2)}) collective-permute-start(bf16[13,32,256]{2,1,0:T(8,128)(2,1)S(1)} %collective-permute-done.9.near2), channel_id=1, source_target_pairs={{0,1},{1,0},{2,3},{3,2},{4,5},{5,4},{6,7},{7,6},{8,9},{9,8},{10,11... | collective-permute-start | bytes 638984 | tf_op jit(solution)/shard_map/ppermute | solution.py:129
  72.7 0.3 collective-permute-done.8.near1
  73.0 2.6 %collective-permute-start.12 = (bf16[13,32,256]{2,1,0:T(8,128)(2,1)S(1)}, bf16[13,32,256]{2,1,0:T(8,128)(2,1)S(1)}, u32[]{:S(2)}, u32[]{:S(2)}) collective-permute-start(bf16[13,32,256]{2,1,0:T(8,128)(2,1)S(1)} %collective-permute-done.8.near1), channel_id=1, source_target_pairs={{0,1},{1,0},{2,3},{3,2},{4,5},{5,4},{6,7},{7,6},{8,9},{9,8},{10,11... | collective-permute-start | bytes 638984 | tf_op jit(solution)/shard_map/ppermute | solution.py:129
  75.6 0.0 collective-permute-done.11.far
  75.6 5.2 %collective-permute-start.15 = (bf16[7,32,256]{2,1,0:T(8,128)(2,1)S(1)}, bf16[7,32,256]{2,1,0:T(8,128)(2,1)S(1)}, u32[]{:S(2)}, u32[]{:S(2)}) collective-permute-start(bf16[7,32,256]{2,1,0:T(8,128)(2,1)S(1)} %collective-permute-done.11.far), channel_id=1, source_target_pairs={{0,1},{1,0},{2,3},{3,2},{4,5},{5,4},{6,7},{7,6},{8,9},{9,8},{10,11... | collective-permute-start | bytes 344072 | tf_op jit(solution)/shard_map/ppermute | solution.py:129
  80.8 0.6 pad_add_fusion.where_ref
  81.4 0.4 collective-permute-done.15.swap4
  81.8 0.0 collective-permute-done.14.swap3
  81.8 0.0 collective-permute-done.13.swap2
  81.8 0.0 collective-permute-done.12.swap1
  81.8 0.0 all-to-all-done.1.cols
  81.8 0.0 copy-done.1
  81.8 0.0 copy-start
  81.8 2.3 %copy-done = bf16[1536,1536]{1,0:T(8,128)(2,1)S(1)} copy-done((bf16[1536,1536]{1,0:T(8,128)(2,1)S(1)}, bf16[1536,1536]{1,0:T(8,128)(2,1)}, u32[]{:S(2)}) %copy-start) | copy-done | bytes 4718616
  84.1 0.0 copy-start.2
  84.1 0.6 copy-done.2
  84.7 9.1 %shard_map.41 = (bf16[1536,1536]{1,0:T(8,128)(2,1)}, bf16[1536,512]{1,0:T(8,128)(2,1)}) custom-call(s32[2]{0:T(128)S(1)} %copy-done.2, bf16[1536,1536]{1,0:T(8,128)(2,1)S(1)} %copy-done, bf16[2,256,256]{2,1,0:T(8,128)(2,1)S(1)} %copy-done.1, bf16[13,32,256]{2,1,0:T(8,128)(2,1)S(1)} %pad_maximum_fusion.own, ...), custom_call_target="tpu_custom_call" | custom-call | flops 2415919104 | bytes 9437184 | tf_op jit(solution)/shard_map/pallas_call | solution.py:89
  (8 shorter events, 0.1 us)
Async XLA Ops:
  1.9 4.0 %collective-permute-start = (bf16[6,32,256]{2,1,0:T(8,128)(2,1)S(1)}, bf16[6,32,256]{2,1,0:T(8,128)(2,1)S(1)}, u32[]{:S(2)}, u32[]{:S(2)}) collective-permute-start(bf16[6,32,256]{2,1,0:T(8,128)(2,1)S(1)} %get-tuple-element.2), channel_id=1, source_target_pairs={{0,2},{1,3},{16,18},{17,19},{32,34},{33,35},{48,50},{49,51},{64,66... | collective-permute-start | bytes 294920 | tf_op jit(solution)/shard_map/ppermute | solution.py:129
  2.6 4.0 %collective-permute-start.5 = (bf16[6,32,256]{2,1,0:T(8,128)(2,1)S(1)}, bf16[6,32,256]{2,1,0:T(8,128)(2,1)S(1)}, u32[]{:S(2)}, u32[]{:S(2)}) collective-permute-start(bf16[6,32,256]{2,1,0:T(8,128)(2,1)S(1)} %get-tuple-element.3), channel_id=1, source_target_pairs={{0,10},{1,11},{16,26},{17,27},{32,42},{33,43},{48,58},{49,59},{64,... | collective-permute-start | bytes 294920 | tf_op jit(solution)/shard_map/ppermute | solution.py:129
  3.2 4.0 %collective-permute-start.4 = (bf16[6,32,256]{2,1,0:T(8,128)(2,1)S(1)}, bf16[6,32,256]{2,1,0:T(8,128)(2,1)S(1)}, u32[]{:S(2)}, u32[]{:S(2)}) collective-permute-start(bf16[6,32,256]{2,1,0:T(8,128)(2,1)S(1)} %get-tuple-element.4), channel_id=1, source_target_pairs={{0,12},{1,13},{16,28},{17,29},{32,44},{33,45},{48,60},{49,61},{64,... | collective-permute-start | bytes 294920 | tf_op jit(solution)/shard_map/ppermute | solution.py:129
  3.9 3.4 %collective-permute-start.3 = (bf16[6,32,256]{2,1,0:T(8,128)(2,1)S(1)}, bf16[6,32,256]{2,1,0:T(8,128)(2,1)S(1)}, u32[]{:S(2)}, u32[]{:S(2)}) collective-permute-start(bf16[6,32,256]{2,1,0:T(8,128)(2,1)S(1)} %get-tuple-element.5), channel_id=1, source_target_pairs={{0,14},{1,15},{16,30},{17,31},{32,46},{33,47},{48,62},{49,63},{64,... | collective-permute-start | bytes 294920 | tf_op jit(solution)/shard_map/ppermute | solution.py:129
  4.6 11.2 %collective-permute-start.2 = (bf16[6,32,256]{2,1,0:T(8,128)(2,1)S(1)}, bf16[6,32,256]{2,1,0:T(8,128)(2,1)S(1)}, u32[]{:S(2)}, u32[]{:S(2)}) collective-permute-start(bf16[6,32,256]{2,1,0:T(8,128)(2,1)S(1)} %get-tuple-element.6), channel_id=1, source_target_pairs={{0,6},{1,7},{16,22},{17,23},{32,38},{33,39},{48,54},{49,55},{64,70... | collective-permute-start | bytes 294920 | tf_op jit(solution)/shard_map/ppermute | solution.py:129
  5.9 9.9 %collective-permute-start.1 = (bf16[6,32,256]{2,1,0:T(8,128)(2,1)S(1)}, bf16[6,32,256]{2,1,0:T(8,128)(2,1)S(1)}, u32[]{:S(2)}, u32[]{:S(2)}) collective-permute-start(bf16[6,32,256]{2,1,0:T(8,128)(2,1)S(1)} %get-tuple-element.7), channel_id=1, source_target_pairs={{0,4},{1,5},{16,20},{17,21},{32,36},{33,37},{48,52},{49,53},{64,68... | collective-permute-start | bytes 294920 | tf_op jit(solution)/shard_map/ppermute | solution.py:129
  6.6 9.2 %collective-permute-start.6 = (bf16[6,32,256]{2,1,0:T(8,128)(2,1)S(1)}, bf16[6,32,256]{2,1,0:T(8,128)(2,1)S(1)}, u32[]{:S(2)}, u32[]{:S(2)}) collective-permute-start(bf16[6,32,256]{2,1,0:T(8,128)(2,1)S(1)} %get-tuple-element.8), channel_id=1, source_target_pairs={{0,8},{1,9},{16,24},{17,25},{32,40},{33,41},{48,56},{49,57},{64,72... | collective-permute-start | bytes 294920 | tf_op jit(solution)/shard_map/ppermute | solution.py:129
  16.5 18.3 %all-to-all-start = ((bf16[16,32,256]{2,1,0:T(8,128)(2,1)}), bf16[16,32,256]{2,1,0:T(8,128)(2,1)S(1)}, u32[]{:S(2)}, u32[]{:S(2)}) async-start(bf16[16,32,256]{2,1,0:T(8,128)(2,1)} %broadcast_in_dim.19), calls=%async_computation | async-start | bytes 524288 | tf_op jit(solution)/shard_map/all_to_all | solution.py:140
  23.5 11.3 %collective-permute-start.16 = (bf16[6,32,256]{2,1,0:T(8,128)(2,1)S(1)}, bf16[6,32,256]{2,1,0:T(8,128)(2,1)S(1)}, u32[]{:S(2)}, u32[]{:S(2)}) collective-permute-start(bf16[6,32,256]{2,1,0:T(8,128)(2,1)S(1)} %fusion.8), channel_id=1, source_target_pairs={{0,0},{1,16},{2,32},{3,48},{4,64},{5,80},{6,96},{7,112},{8,128},{9... | collective-permute-start | bytes 294920 | tf_op jit(solution)/shard_map/ppermute | solution.py:129
  36.1 45.7 %copy-start.1 = (bf16[2,256,256]{2,1,0:T(8,128)(2,1)S(1)}, bf16[2,256,256]{2,1,0:T(8,128)(2,1)}, u32[]{:S(2)}) copy-start(bf16[2,256,256]{2,1,0:T(8,128)(2,1)} %inverses.1) | copy-start | bytes 786436
  36.1 45.6 %all-to-all-start.1 = ((bf16[16,6,32,256]{3,2,1,0:T(8,128)(2,1)}), bf16[16,6,32,256]{3,2,1,0:T(8,128)(2,1)S(1)}, u32[]{:S(2)}, u32[]{:S(2)}) async-start(bf16[16,6,32,256]{3,2,1,0:T(8,128)(2,1)} %broadcast_in_dim.20), calls=%async_computation.1 | async-start | bytes 3145728 | tf_op jit(solution)/shard_map/all_to_all | solution.py:150
  50.3 2.1 %collective-permute-start.7 = (bf16[7,32,256]{2,1,0:T(8,128)(2,1)S(1)}, bf16[7,32,256]{2,1,0:T(8,128)(2,1)S(1)}, u32[]{:S(2)}, u32[]{:S(2)}) collective-permute-start(bf16[7,32,256]{2,1,0:T(8,128)(2,1)S(1)} %pad_maximum_fusion.1), channel_id=1, source_target_pairs={{0,1},{1,0},{2,3},{3,2},{4,5},{5,4},{6,7},{7,6},{8,9},{9,8},{10,11... | collective-permute-start | bytes 344072 | tf_op jit(solution)/shard_map/ppermute | solution.py:129
  52.4 11.3 %collective-permute-start.10 = (bf16[13,32,256]{2,1,0:T(8,128)(2,1)S(1)}, bf16[13,32,256]{2,1,0:T(8,128)(2,1)S(1)}, u32[]{:S(2)}, u32[]{:S(2)}) collective-permute-start(bf16[13,32,256]{2,1,0:T(8,128)(2,1)S(1)} %pad_maximum_fusion.own), channel_id=1, source_target_pairs={{0,10},{1,7},{2,12},{3,9},{4,14},{5,11},{6,0},{7,13},{8,2},{9,15},... | collective-permute-start | bytes 638984 | tf_op jit(solution)/shard_map/ppermute | solution.py:129
  53.8 17.0 %collective-permute-start.9 = (bf16[13,32,256]{2,1,0:T(8,128)(2,1)S(1)}, bf16[13,32,256]{2,1,0:T(8,128)(2,1)S(1)}, u32[]{:S(2)}, u32[]{:S(2)}) collective-permute-start(bf16[13,32,256]{2,1,0:T(8,128)(2,1)S(1)} %pad_maximum_fusion.own), channel_id=1, source_target_pairs={{0,12},{1,5},{2,14},{3,7},{4,0},{5,9},{6,2},{7,11},{8,4},{9,13},{1... | collective-permute-start | bytes 638984 | tf_op jit(solution)/shard_map/ppermute | solution.py:129
  59.4 13.6 %collective-permute-start.8 = (bf16[13,32,256]{2,1,0:T(8,128)(2,1)S(1)}, bf16[13,32,256]{2,1,0:T(8,128)(2,1)S(1)}, u32[]{:S(2)}, u32[]{:S(2)}) collective-permute-start(bf16[13,32,256]{2,1,0:T(8,128)(2,1)S(1)} %pad_maximum_fusion.own), channel_id=1, source_target_pairs={{0,14},{1,3},{2,0},{3,5},{4,2},{5,7},{6,4},{7,9},{8,6},{9,11},{10,... | collective-permute-start | bytes 638984 | tf_op jit(solution)/shard_map/ppermute | solution.py:129
  59.4 16.2 %collective-permute-start.11 = (bf16[7,32,256]{2,1,0:T(8,128)(2,1)S(1)}, bf16[7,32,256]{2,1,0:T(8,128)(2,1)S(1)}, u32[]{:S(2)}, u32[]{:S(2)}) collective-permute-start(bf16[7,32,256]{2,1,0:T(8,128)(2,1)S(1)} %pad_maximum_fusion.2), channel_id=1, source_target_pairs={{0,8},{1,9},{2,10},{3,11},{4,12},{5,13},{6,14},{7,15},{8,0},{9,1},... | collective-permute-start | bytes 344072 | tf_op jit(solution)/shard_map/ppermute | solution.py:129
  63.7 18.0 %collective-permute-start.14 = (bf16[13,32,256]{2,1,0:T(8,128)(2,1)S(1)}, bf16[13,32,256]{2,1,0:T(8,128)(2,1)S(1)}, u32[]{:S(2)}, u32[]{:S(2)}) collective-permute-start(bf16[13,32,256]{2,1,0:T(8,128)(2,1)S(1)} %collective-permute-done.10.near3), channel_id=1, source_target_pairs={{0,1},{1,0},{2,3},{3,2},{4,5},{5,4},{6,7},{7,6},{8,9},{9,8},{10,11... | collective-permute-start | bytes 638984 | tf_op jit(solution)/shard_map/ppermute | solution.py:129
  70.8 11.0 %collective-permute-start.13 = (bf16[13,32,256]{2,1,0:T(8,128)(2,1)S(1)}, bf16[13,32,256]{2,1,0:T(8,128)(2,1)S(1)}, u32[]{:S(2)}, u32[]{:S(2)}) collective-permute-start(bf16[13,32,256]{2,1,0:T(8,128)(2,1)S(1)} %collective-permute-done.9.near2), channel_id=1, source_target_pairs={{0,1},{1,0},{2,3},{3,2},{4,5},{5,4},{6,7},{7,6},{8,9},{9,8},{10,11... | collective-permute-start | bytes 638984 | tf_op jit(solution)/shard_map/ppermute | solution.py:129
  73.0 8.7 %collective-permute-start.12 = (bf16[13,32,256]{2,1,0:T(8,128)(2,1)S(1)}, bf16[13,32,256]{2,1,0:T(8,128)(2,1)S(1)}, u32[]{:S(2)}, u32[]{:S(2)}) collective-permute-start(bf16[13,32,256]{2,1,0:T(8,128)(2,1)S(1)} %collective-permute-done.8.near1), channel_id=1, source_target_pairs={{0,1},{1,0},{2,3},{3,2},{4,5},{5,4},{6,7},{7,6},{8,9},{9,8},{10,11... | collective-permute-start | bytes 638984 | tf_op jit(solution)/shard_map/ppermute | solution.py:129
  75.6 6.2 %collective-permute-start.15 = (bf16[7,32,256]{2,1,0:T(8,128)(2,1)S(1)}, bf16[7,32,256]{2,1,0:T(8,128)(2,1)S(1)}, u32[]{:S(2)}, u32[]{:S(2)}) collective-permute-start(bf16[7,32,256]{2,1,0:T(8,128)(2,1)S(1)} %collective-permute-done.11.far), channel_id=1, source_target_pairs={{0,1},{1,0},{2,3},{3,2},{4,5},{5,4},{6,7},{7,6},{8,9},{9,8},{10,11... | collective-permute-start | bytes 344072 | tf_op jit(solution)/shard_map/ppermute | solution.py:129
  81.8 2.3 %copy-start = (bf16[1536,1536]{1,0:T(8,128)(2,1)S(1)}, bf16[1536,1536]{1,0:T(8,128)(2,1)}, u32[]{:S(2)}) copy-start(bf16[1536,1536]{1,0:T(8,128)(2,1)} %matrix.1) | copy-start | bytes 14155780
  84.1 0.6 copy-start.2

commit v2 on v1

v2 whole, which is shorter than its diff:
```python
import jax
import jax.numpy as jnp
from jax import lax
from jax.experimental import pallas as pl
from jax.experimental.pallas import tpu as pltpu
from jax.sharding import PartitionSpec as P

BOTH = ("row", "col")
NB = 256
SLOTS = 6
SIDE = 16
LINE = 8
CUT = NB // LINE
PIECE = SLOTS * CUT

SMEM = pl.BlockSpec(memory_space=pltpu.SMEM)
VMEM = pl.BlockSpec(memory_space=pltpu.VMEM)
HBM = pl.BlockSpec(memory_space=pltpu.HBM)
ANY = pl.BlockSpec(memory_space=pl.ANY)
MIB = 1024 * 1024


def ring(a, b, n):
    return min((a - b) % n, (b - a) % n)


def targets():
    table = []
    for rank in range(SIDE):
        def depth(q):
            return ring(q // 2, rank // 2, LINE)

        def spread(k):
            return ring(k // 4, rank // 4, 4) + ring(k % 4, rank % 4, 4)

        pieces = sorted(range(SIDE), key=lambda q: (-depth(q), q))
        places = sorted(range(SIDE), key=lambda k: (spread(k), (k - rank) % SIDE))
        row = [0] * SIDE
        for q, k in zip(pieces, places):
            row[q] = k
        table.append(row)
    return table


TARGETS = targets()
LEFT, RIGHT = pl.ds(0, NB), pl.ds(NB, NB)


def dot_t(left, right):
    return lax.dot_general(
        left, right, (((1,), (1,)), ((), ())), preferred_element_type=jnp.float32
    )


def keep(f, columns, rank, least):
    @pl.when(rank < least)
    def _():
        f[pl.ds(0, NB), columns] = jnp.zeros((NB, NB), jnp.bfloat16)


def factor(f, raw0, raw1, pivot, inv, rank):
    f[:, LEFT] = dot_t(raw0, inv[0]).astype(jnp.bfloat16)
    keep(f, LEFT, rank, 1)
    head = (raw1.astype(jnp.float32) - dot_t(f[:, LEFT], pivot)).astype(jnp.bfloat16)
    f[:, RIGHT] = dot_t(head, inv[1]).astype(jnp.bfloat16)
    keep(f, RIGHT, rank, 2)


def finish_kernel(order_ref, inv, own, near1, near2, near3, swap1, swap2, swap3, far, swap4, cols, matrix,
                  factored, panels, held, edge, rows_x, cols_x, base, rows_f, cols_f, sem_m, sem_e, sem_o):
    row, col = lax.axis_index("row"), lax.axis_index("col")
    z, core = col // 2, lax.rem(col, 2)
    edges = [pltpu.make_async_copy(src, edge.at[i], sem_e.at[i]) for i, src in enumerate((far, swap4))]
    for c in edges:
        c.start()
    loads = []
    for b in range(SLOTS):
        loads.append(pltpu.make_async_copy(matrix.at[pl.ds(NB * b, NB)], held.at[b], sem_m.at[b]))
        loads[b].start()

    def place(msg, slot):
        for h in range(2):
            rows_x[h, :, slot] = msg[pl.ds(PIECE * h, PIECE)].reshape(SLOTS, CUT, NB)
        base[slot] = msg[pl.ds(2 * PIECE, CUT)]

    place(own, z)
    for d, (near, swap) in enumerate(((near1, swap1), (near2, swap2), (near3, swap3)), 1):
        up, down = lax.rem(z + d, LINE), lax.rem(z + LINE - d, LINE)
        place(near, jnp.where(core == 0, up, down))
        place(swap, jnp.where(core == 0, down, up))
    for s in range(LINE):
        for h in range(2):
            cols_x[h, :, s] = cols[order_ref[col * SIDE + 2 * s + h]].reshape(SLOTS, CUT, NB)
    for c in edges:
        c.wait()
    across = lax.rem(z + LINE // 2, LINE)
    rows_x[core, :, across] = edge[0, pl.ds(0, PIECE)].reshape(SLOTS, CUT, NB)
    rows_x[1 - core, :, across] = edge[1, pl.ds(0, PIECE)].reshape(SLOTS, CUT, NB)
    base[across] = edge[0, pl.ds(PIECE, CUT)]
    pivot = dot_t(base[...].reshape(NB, NB), inv[0]).astype(jnp.bfloat16)
    factor(rows_f, rows_x[0].reshape(SLOTS * NB, NB), rows_x[1].reshape(SLOTS * NB, NB), pivot, inv, row)
    stores = [pltpu.make_async_copy(rows_f, panels, sem_o.at[SLOTS])]
    stores[0].start()
    factor(cols_f, cols_x[0].reshape(SLOTS * NB, NB), cols_x[1].reshape(SLOTS * NB, NB), pivot, inv, col)
    for b in range(SLOTS):
        loads[b].wait()
        at = pl.ds(NB * b, NB)
        value = held[b].astype(jnp.float32) - dot_t(rows_f[at, :], cols_f[...])
        held[b] = value.astype(jnp.bfloat16)
        stores.append(pltpu.make_async_copy(held.at[b], factored.at[at], sem_o.at[b]))
        stores[-1].start()
    for c in stores:
        c.wait()


def finish(inverses, own, near, swaps, far, cols, matrix):
    rows, columns = matrix.shape
    matrix = pltpu.with_memory_space_constraint(matrix, pltpu.HBM)
    return pl.pallas_call(
        finish_kernel,
        out_shape=(
            jax.ShapeDtypeStruct(matrix.shape, jnp.bfloat16),
            jax.ShapeDtypeStruct((rows, 2 * NB), jnp.bfloat16),
        ),
        in_specs=[SMEM] + [VMEM] * 8 + [ANY, ANY, VMEM, HBM],
        out_specs=(HBM, HBM),
        scratch_shapes=[
            pltpu.VMEM((SLOTS, NB, columns), jnp.bfloat16),
            pltpu.VMEM((2,) + far.shape, jnp.bfloat16),
            pltpu.VMEM((2, SLOTS, LINE, CUT, NB), jnp.bfloat16),
            pltpu.VMEM((2, SLOTS, LINE, CUT, NB), jnp.bfloat16),
            pltpu.VMEM((LINE, CUT, NB), jnp.bfloat16),
            pltpu.VMEM((rows, 2 * NB), jnp.bfloat16),
            pltpu.VMEM((columns, 2 * NB), jnp.bfloat16),
            pltpu.SemaphoreType.DMA((SLOTS,)),
            pltpu.SemaphoreType.DMA((2,)),
            pltpu.SemaphoreType.DMA((SLOTS + 1,)),
        ],
        compiler_params=pltpu.CompilerParams(vmem_limit_bytes=36 * MIB),
        cost_estimate=pl.CostEstimate(
            flops=2 * rows * columns * 2 * NB, bytes_accessed=4 * rows * columns, transcendentals=0
        ),
    )(jnp.asarray(TARGETS, jnp.int32).reshape(-1), inverses, own, *near, *swaps[:3], far, swaps[3], cols, matrix)


def moves(step):
    pairs = []
    for row in range(SIDE):
        for z in range(LINE):
            for core in range(2):
                to = step(row, z, core)
                if to is not None:
                    pairs.append((row * SIDE + 2 * z + core, to[0] * SIDE + 2 * (to[1] % LINE) + to[2]))
    return pairs


def send(value, pairs):
    return lax.ppermute(value, BOTH, pairs)


def shared(piece, axis, groups):
    copies = len(groups[0])
    spread = jnp.broadcast_to(piece[None], (copies,) + piece.shape).reshape(-1, NB)
    return lax.all_to_all(spread, axis, 0, 0, tiled=True, axis_index_groups=groups).reshape(
        (copies,) + piece.shape)


PLANE = [list(range(SIDE))]
LINES = [[2 * z + h for z in range(LINE)] for h in range(2)]


def shards(matrix, inverses):
    row, col = lax.axis_index("row"), lax.axis_index("col")
    z = col // 2
    cut = matrix[:, :NB].reshape(SLOTS, LINE, CUT, NB)
    mine = jnp.where(z == 0, cut[:, 0], 0)
    for d in (1, 5, 6, 7, 3, 2, 4):
        mine = mine + send(cut[:, d], moves(lambda r, zz, h: (r, d, h) if zz == 0 else None))
    mine = mine.reshape(PIECE, NB)
    crossed = send(mine, [(r * SIDE + q, TARGETS[r][q] * SIDE + r) for r in range(SIDE) for q in range(SIDE)])
    head = shared(mine[:CUT], "row", PLANE)[1]
    over = moves(lambda r, zz, h: (r, zz, 1 - h))
    theirs = send(jnp.concatenate([mine, head]), over)
    is0 = col % 2 == 0
    own = jnp.concatenate([
        jnp.where(is0, mine, theirs[:PIECE]),
        jnp.where(is0, theirs[:PIECE], mine),
        jnp.where(is0, head, theirs[PIECE:]),
    ])
    near = [send(own, moves(lambda r, zz, h: (r, zz - d if h == 0 else zz + d, h))) for d in (1, 2, 3)]
    far = send(jnp.concatenate([mine, own[2 * PIECE:]]), moves(lambda r, zz, h: (r, zz + LINE // 2, h)))
    cols = shared(crossed, "row", PLANE)
    swaps = [send(v, over) for v in (*near, far)]
    return finish(inverses, own, near, swaps, far, cols, matrix)


def solution(mesh):
    return jax.shard_map(
        shards,
        mesh=mesh,
        in_specs=(P("row", "col"), P()),
        out_specs=(P("row", "col"), P("row", None)),
        check_vma=False,
    )
```

time: 94.5 us -> 87.7 us (0.928)
  starting transfers between devices: 58.5 us -> 48.8 us
  waiting for transfers between devices: 18.4 us -> 24.3 us
  local copies, waits for them, and re-layouts: 6.25 us -> 3.95 us
    ppermute x17, starting transfers between devices: 37.5 us -> 29.5 us  [send(): return lax.ppermute(value, BOTH, pairs)]
    ppermute x17, waiting for transfers between devices: 18.4 us -> 24.3 us  [send(): return lax.ppermute(value, BOTH, pairs)]
    unnamed x6 -> x4, local copies, waits for them, and re-layouts: 2.94 us -> 0.68 us
    all_to_all x2, starting transfers between devices: 21 us -> 19.3 us  [shared(): lax.all_to_all(spread, axis, 0, 0, tiled=True, axis_index_groups=groups)]
  transfers between devices with their start and end apart: 19 -> 19, of which waited for: 6 -> 7; matrix products, arithmetic and copies ran while one was open for 1% -> 0% of each run, Pallas kernels for 0% -> 0%
where the time goes in v2:
time: 87.7 us; the launch traced here: 86.8 us
  starting transfers between devices  48.8 us (56%)
  waiting for transfers between devices  24.3 us (28%)
  Pallas kernels  8.62 us (10%)
  local copies, waits for them, and re-layouts  3.95 us (5%)
  between operations  0.98 us (1%)
    ppermute x17, starting transfers between devices, send(): return lax.ppermute(value, BOTH, pairs)  29.5 us
    ppermute x17, waiting for transfers between devices, send(): return lax.ppermute(value, BOTH, pairs)  24.3 us
    all_to_all x2, starting transfers between devices, shared(): lax.all_to_all(spread, axis, 0, 0, tiled=True, axis_index_groups=groups)  19.3 us
    pallas_call x1, Pallas kernels, finish(): pl.pallas_call(finish_kernel, out_shape=(jax.ShapeDtypeStruct(matrix.shap...  8.62 us
    broadcast_in_dim x3, local copies, waits for them, and re-layouts, shared(): jnp.broadcast_to(piece[None], (copies,) + piece.shape).reshape(-1, NB)  2.03 us
  transfers between devices with their start and end apart: 19, of which 7 were waited for; matrix products, arithmetic and copies ran while one was open for 0% of the time, Pallas kernels for 0%

profile of v2, /device:TPU:99, one launch (start us, length us, event | category | flops | bytes accessed | tf_op | source)
XLA Modules:
  0.0 86.8 jit_solution(1060155314593763984)
XLA Ops:
  0.6 1.2 %slice.45 = bf16[1536,256]{1,0:T(8,128)(2,1)S(1)} slice(bf16[1536,1536]{1,0:T(8,128)(2,1)} %matrix.1), slice={[0:1536], [0:256]} | slice | bytes 1572864 | tf_op jit(solution)/shard_map/slice | solution.py:175
  1.8 0.1 slice_bitcast_fusion.6
  1.9 0.7 collective-permute-start
  2.6 0.7 collective-permute-start.5
  3.2 1.3 %collective-permute-start.4 = (bf16[6,32,256]{2,1,0:T(8,128)(2,1)S(1)}, bf16[6,32,256]{2,1,0:T(8,128)(2,1)S(1)}, u32[]{:S(2)}, u32[]{:S(2)}) collective-permute-start(bf16[6,32,256]{2,1,0:T(8,128)(2,1)S(1)} %get-tuple-element.4), channel_id=1, source_target_pairs={{0,6},{1,7},{16,22},{17,23},{32,38},{33,39},{48,54},{49,55},{64,70... | collective-permute-start | bytes 294920 | tf_op jit(solution)/shard_map/ppermute | solution.py:158
  4.5 0.7 collective-permute-start.3
  5.2 0.7 collective-permute-start.2
  5.9 0.0 collective-permute-done
  5.9 0.7 collective-permute-start.1
  6.6 0.0 collective-permute-done.5
  6.6 0.7 collective-permute-start.6
  7.3 3.8 %collective-permute-done.4 = bf16[6,32,256]{2,1,0:T(8,128)(2,1)S(1)} collective-permute-done((bf16[6,32,256]{2,1,0:T(8,128)(2,1)S(1)}, bf16[6,32,256]{2,1,0:T(8,128)(2,1)S(1)}, u32[]{:S(2)}, u32[]{:S(2)}) %collective-permute-start.4) | collective-permute-done | bytes 98336 | tf_op jit(solution)/shard_map/ppermute | solution.py:158
  11.1 0.0 collective-permute-done.3
  11.1 0.0 collective-permute-done.2
  11.1 0.0 collective-permute-done.1
  11.1 0.0 collective-permute-done.6
  11.1 0.7 broadcast_in_dim.20
  11.9 6.9 %all-to-all-start = ((bf16[16,32,256]{2,1,0:T(8,128)(2,1)}), bf16[16,32,256]{2,1,0:T(8,128)(2,1)S(1)}, u32[]{:S(2)}, u32[]{:S(2)}) async-start(bf16[16,32,256]{2,1,0:T(8,128)(2,1)} %broadcast_in_dim.20), calls=%async_computation | async-start | bytes 524288 | tf_op jit(solution)/shard_map/all_to_all | solution.py:164
  18.8 7.3 %collective-permute-start.16 = (bf16[192,256]{1,0:T(8,128)(2,1)S(1)}, bf16[192,256]{1,0:T(8,128)(2,1)S(1)}, u32[]{:S(2)}, u32[]{:S(2)}) collective-permute-start(bf16[192,256]{1,0:T(8,128)(2,1)S(1)} %bitcast.76), channel_id=1, source_target_pairs={{0,224},{1,160},{2,240},{3,96},{4,80},{5,112},{6,48},{7,64},{8,0},... | collective-permute-start | bytes 294920 | tf_op jit(solution)/shard_map/ppermute | solution.py:158
  26.1 5.8 %collective-permute-done.16 = bf16[192,256]{1,0:T(8,128)(2,1)S(1)} collective-permute-done((bf16[192,256]{1,0:T(8,128)(2,1)S(1)}, bf16[192,256]{1,0:T(8,128)(2,1)S(1)}, u32[]{:S(2)}, u32[]{:S(2)}) %collective-permute-start.16) | collective-permute-done | bytes 98336 | tf_op jit(solution)/shard_map/ppermute | solution.py:158
  32.0 0.0 all-to-all-done
  32.0 1.3 %broadcast_in_dim.21 = bf16[16,192,256]{2,1,0:T(8,128)(2,1)} broadcast(bf16[192,256]{1,0:T(8,128)(2,1)S(1)} %collective-permute-done.16), dimensions={1,2} | broadcast | bytes 1671168 | tf_op jit(solution)/shard_map/broadcast_in_dim | solution.py:163
  33.3 0.0 copy-start
  33.3 12.4 %all-to-all-start.1 = ((bf16[16,192,256]{2,1,0:T(8,128)(2,1)}), bf16[16,192,256]{2,1,0:T(8,128)(2,1)S(1)}, u32[]{:S(2)}, u32[]{:S(2)}) async-start(bf16[16,192,256]{2,1,0:T(8,128)(2,1)} %broadcast_in_dim.21), calls=%async_computation.1 | async-start | bytes 3145728 | tf_op jit(solution)/shard_map/all_to_all | solution.py:164
  45.7 1.0 %collective-permute-start.7 = (bf16[224,256]{1,0:T(8,128)(2,1)S(1)}, bf16[224,256]{1,0:T(8,128)(2,1)S(1)}, u32[]{:S(2)}, u32[]{:S(2)}) collective-permute-start(bf16[224,256]{1,0:T(8,128)(2,1)S(1)} %pad_maximum_fusion.1), channel_id=1, source_target_pairs={{0,1},{1,0},{2,3},{3,2},{4,5},{5,4},{6,7},{7,6},{8,9},{9,8},{10,11... | collective-permute-start | bytes 344072 | tf_op jit(solution)/shard_map/ppermute | solution.py:158
  46.7 1.0 %collective-permute-done.7 = bf16[224,256]{1,0:T(8,128)(2,1)S(1)} collective-permute-done((bf16[224,256]{1,0:T(8,128)(2,1)S(1)}, bf16[224,256]{1,0:T(8,128)(2,1)S(1)}, u32[]{:S(2)}, u32[]{:S(2)}) %collective-permute-start.7) | collective-permute-done | bytes 114720 | tf_op jit(solution)/shard_map/ppermute | solution.py:158
  47.7 5.4 %collective-permute-start.10 = (bf16[416,256]{1,0:T(8,128)(2,1)S(1)}, bf16[416,256]{1,0:T(8,128)(2,1)S(1)}, u32[]{:S(2)}, u32[]{:S(2)}) collective-permute-start(bf16[416,256]{1,0:T(8,128)(2,1)S(1)} %pad_maximum_fusion.own), channel_id=1, source_target_pairs={{0,10},{1,7},{2,12},{3,9},{4,14},{5,11},{6,0},{7,13},{8,2},{9,15},... | collective-permute-start | bytes 638984 | tf_op jit(solution)/shard_map/ppermute | solution.py:158
  53.1 0.5 collective-permute-start.9
  53.5 0.3 collective-permute-start.8
  53.8 5.3 %collective-permute-start.14 = (bf16[224,256]{1,0:T(8,128)(2,1)S(1)}, bf16[224,256]{1,0:T(8,128)(2,1)S(1)}, u32[]{:S(2)}, u32[]{:S(2)}) collective-permute-start(bf16[224,256]{1,0:T(8,128)(2,1)S(1)} %pad_maximum_fusion.2), channel_id=1, source_target_pairs={{0,8},{1,9},{2,10},{3,11},{4,12},{5,13},{6,14},{7,15},{8,0},{9,1},... | collective-permute-start | bytes 344072 | tf_op jit(solution)/shard_map/ppermute | solution.py:158
  59.1 2.7 %collective-permute-done.10.near3 = bf16[416,256]{1,0:T(8,128)(2,1)S(1)} collective-permute-done((bf16[416,256]{1,0:T(8,128)(2,1)S(1)}, bf16[416,256]{1,0:T(8,128)(2,1)S(1)}, u32[]{:S(2)}, u32[]{:S(2)}) %collective-permute-start.10) | collective-permute-done | bytes 213024 | tf_op jit(solution)/shard_map/ppermute | solution.py:158
  61.7 0.0 collective-permute-start.13
  61.7 6.4 %collective-permute-done.9.near2 = bf16[416,256]{1,0:T(8,128)(2,1)S(1)} collective-permute-done((bf16[416,256]{1,0:T(8,128)(2,1)S(1)}, bf16[416,256]{1,0:T(8,128)(2,1)S(1)}, u32[]{:S(2)}, u32[]{:S(2)}) %collective-permute-start.9) | collective-permute-done | bytes 213024 | tf_op jit(solution)/shard_map/ppermute | solution.py:158
  68.1 0.0 collective-permute-start.12
  68.1 3.7 %collective-permute-done.8.near1 = bf16[416,256]{1,0:T(8,128)(2,1)S(1)} collective-permute-done((bf16[416,256]{1,0:T(8,128)(2,1)S(1)}, bf16[416,256]{1,0:T(8,128)(2,1)S(1)}, u32[]{:S(2)}, u32[]{:S(2)}) %collective-permute-start.8) | collective-permute-done | bytes 213024 | tf_op jit(solution)/shard_map/ppermute | solution.py:158
  71.8 0.0 collective-permute-start.11
  71.8 0.0 collective-permute-done.14.far
  71.8 4.5 %collective-permute-start.15 = (bf16[224,256]{1,0:T(8,128)(2,1)S(1)}, bf16[224,256]{1,0:T(8,128)(2,1)S(1)}, u32[]{:S(2)}, u32[]{:S(2)}) collective-permute-start(bf16[224,256]{1,0:T(8,128)(2,1)S(1)} %collective-permute-done.14.far), channel_id=1, source_target_pairs={{0,1},{1,0},{2,3},{3,2},{4,5},{5,4},{6,7},{7,6},{8,9},{9,8},{10,11... | collective-permute-start | bytes 344072 | tf_op jit(solution)/shard_map/ppermute | solution.py:158
  76.3 1.0 %collective-permute-done.15.swap4 = bf16[224,256]{1,0:T(8,128)(2,1)S(1)} collective-permute-done((bf16[224,256]{1,0:T(8,128)(2,1)S(1)}, bf16[224,256]{1,0:T(8,128)(2,1)S(1)}, u32[]{:S(2)}, u32[]{:S(2)}) %collective-permute-start.15) | collective-permute-done | bytes 114720 | tf_op jit(solution)/shard_map/ppermute | solution.py:158
  77.3 0.0 collective-permute-done.13.swap3
  77.3 0.0 collective-permute-done.12.swap2
  77.3 0.0 collective-permute-done.11.swap1
  77.3 0.0 all-to-all-done.1.cols
  77.3 0.0 copy-done
  77.3 0.0 copy-start.1
  77.3 0.7 copy-done.1
  78.0 8.6 %shard_map.50 = (bf16[1536,1536]{1,0:T(8,128)(2,1)}, bf16[1536,512]{1,0:T(8,128)(2,1)}) custom-call(s32[256]{0:T(256)S(1)} %copy-done.1, bf16[2,256,256]{2,1,0:T(8,128)(2,1)S(1)} %copy-done, bf16[416,256]{1,0:T(8,128)(2,1)S(1)} %pad_maximum_fusion.own, bf16[416,256]{1,0:T(8,128)(2,1)S(1)} %collective-permute-done.8.near1, ...), custom_call_target="tpu_custom_call" | custom-call | flops 2415919104 | bytes 9437184 | tf_op jit(solution)/shard_map/pallas_call | solution.py:119
  (8 shorter events, 0.1 us)
Async XLA Ops:
  1.9 4.0 %collective-permute-start = (bf16[6,32,256]{2,1,0:T(8,128)(2,1)S(1)}, bf16[6,32,256]{2,1,0:T(8,128)(2,1)S(1)}, u32[]{:S(2)}, u32[]{:S(2)}) collective-permute-start(bf16[6,32,256]{2,1,0:T(8,128)(2,1)S(1)} %get-tuple-element.2), channel_id=1, source_target_pairs={{0,2},{1,3},{16,18},{17,19},{32,34},{33,35},{48,50},{49,51},{64,66... | collective-permute-start | bytes 294920 | tf_op jit(solution)/shard_map/ppermute | solution.py:158
  2.6 4.0 %collective-permute-start.5 = (bf16[6,32,256]{2,1,0:T(8,128)(2,1)S(1)}, bf16[6,32,256]{2,1,0:T(8,128)(2,1)S(1)}, u32[]{:S(2)}, u32[]{:S(2)}) collective-permute-start(bf16[6,32,256]{2,1,0:T(8,128)(2,1)S(1)} %get-tuple-element.3), channel_id=1, source_target_pairs={{0,4},{1,5},{16,20},{17,21},{32,36},{33,37},{48,52},{49,53},{64,68... | collective-permute-start | bytes 294920 | tf_op jit(solution)/shard_map/ppermute | solution.py:158
  3.2 7.8 %collective-permute-start.4 = (bf16[6,32,256]{2,1,0:T(8,128)(2,1)S(1)}, bf16[6,32,256]{2,1,0:T(8,128)(2,1)S(1)}, u32[]{:S(2)}, u32[]{:S(2)}) collective-permute-start(bf16[6,32,256]{2,1,0:T(8,128)(2,1)S(1)} %get-tuple-element.4), channel_id=1, source_target_pairs={{0,6},{1,7},{16,22},{17,23},{32,38},{33,39},{48,54},{49,55},{64,70... | collective-permute-start | bytes 294920 | tf_op jit(solution)/shard_map/ppermute | solution.py:158
  4.5 6.5 %collective-permute-start.3 = (bf16[6,32,256]{2,1,0:T(8,128)(2,1)S(1)}, bf16[6,32,256]{2,1,0:T(8,128)(2,1)S(1)}, u32[]{:S(2)}, u32[]{:S(2)}) collective-permute-start(bf16[6,32,256]{2,1,0:T(8,128)(2,1)S(1)} %get-tuple-element.5), channel_id=1, source_target_pairs={{0,14},{1,15},{16,30},{17,31},{32,46},{33,47},{48,62},{49,63},{64,... | collective-permute-start | bytes 294920 | tf_op jit(solution)/shard_map/ppermute | solution.py:158
  5.2 5.9 %collective-permute-start.2 = (bf16[6,32,256]{2,1,0:T(8,128)(2,1)S(1)}, bf16[6,32,256]{2,1,0:T(8,128)(2,1)S(1)}, u32[]{:S(2)}, u32[]{:S(2)}) collective-permute-start(bf16[6,32,256]{2,1,0:T(8,128)(2,1)S(1)} %get-tuple-element.6), channel_id=1, source_target_pairs={{0,12},{1,13},{16,28},{17,29},{32,44},{33,45},{48,60},{49,61},{64,... | collective-permute-start | bytes 294920 | tf_op jit(solution)/shard_map/ppermute | solution.py:158
  5.9 5.2 %collective-permute-start.1 = (bf16[6,32,256]{2,1,0:T(8,128)(2,1)S(1)}, bf16[6,32,256]{2,1,0:T(8,128)(2,1)S(1)}, u32[]{:S(2)}, u32[]{:S(2)}) collective-permute-start(bf16[6,32,256]{2,1,0:T(8,128)(2,1)S(1)} %get-tuple-element.7), channel_id=1, source_target_pairs={{0,10},{1,11},{16,26},{17,27},{32,42},{33,43},{48,58},{49,59},{64,... | collective-permute-start | bytes 294920 | tf_op jit(solution)/shard_map/ppermute | solution.py:158
  6.6 4.5 %collective-permute-start.6 = (bf16[6,32,256]{2,1,0:T(8,128)(2,1)S(1)}, bf16[6,32,256]{2,1,0:T(8,128)(2,1)S(1)}, u32[]{:S(2)}, u32[]{:S(2)}) collective-permute-start(bf16[6,32,256]{2,1,0:T(8,128)(2,1)S(1)} %get-tuple-element.8), channel_id=1, source_target_pairs={{0,8},{1,9},{16,24},{17,25},{32,40},{33,41},{48,56},{49,57},{64,72... | collective-permute-start | bytes 294920 | tf_op jit(solution)/shard_map/ppermute | solution.py:158
  11.9 20.1 %all-to-all-start = ((bf16[16,32,256]{2,1,0:T(8,128)(2,1)}), bf16[16,32,256]{2,1,0:T(8,128)(2,1)S(1)}, u32[]{:S(2)}, u32[]{:S(2)}) async-start(bf16[16,32,256]{2,1,0:T(8,128)(2,1)} %broadcast_in_dim.20), calls=%async_computation | async-start | bytes 524288 | tf_op jit(solution)/shard_map/all_to_all | solution.py:164
  18.8 13.2 %collective-permute-start.16 = (bf16[192,256]{1,0:T(8,128)(2,1)S(1)}, bf16[192,256]{1,0:T(8,128)(2,1)S(1)}, u32[]{:S(2)}, u32[]{:S(2)}) collective-permute-start(bf16[192,256]{1,0:T(8,128)(2,1)S(1)} %bitcast.76), channel_id=1, source_target_pairs={{0,224},{1,160},{2,240},{3,96},{4,80},{5,112},{6,48},{7,64},{8,0},... | collective-permute-start | bytes 294920 | tf_op jit(solution)/shard_map/ppermute | solution.py:158
  33.3 44.0 %copy-start = (bf16[2,256,256]{2,1,0:T(8,128)(2,1)S(1)}, bf16[2,256,256]{2,1,0:T(8,128)(2,1)}, u32[]{:S(2)}) copy-start(bf16[2,256,256]{2,1,0:T(8,128)(2,1)} %inv.1) | copy-start | bytes 786436
  33.3 44.0 %all-to-all-start.1 = ((bf16[16,192,256]{2,1,0:T(8,128)(2,1)}), bf16[16,192,256]{2,1,0:T(8,128)(2,1)S(1)}, u32[]{:S(2)}, u32[]{:S(2)}) async-start(bf16[16,192,256]{2,1,0:T(8,128)(2,1)} %broadcast_in_dim.21), calls=%async_computation.1 | async-start | bytes 3145728 | tf_op jit(solution)/shard_map/all_to_all | solution.py:164
  45.7 2.0 %collective-permute-start.7 = (bf16[224,256]{1,0:T(8,128)(2,1)S(1)}, bf16[224,256]{1,0:T(8,128)(2,1)S(1)}, u32[]{:S(2)}, u32[]{:S(2)}) collective-permute-start(bf16[224,256]{1,0:T(8,128)(2,1)S(1)} %pad_maximum_fusion.1), channel_id=1, source_target_pairs={{0,1},{1,0},{2,3},{3,2},{4,5},{5,4},{6,7},{7,6},{8,9},{9,8},{10,11... | collective-permute-start | bytes 344072 | tf_op jit(solution)/shard_map/ppermute | solution.py:158
  47.7 14.1 %collective-permute-start.10 = (bf16[416,256]{1,0:T(8,128)(2,1)S(1)}, bf16[416,256]{1,0:T(8,128)(2,1)S(1)}, u32[]{:S(2)}, u32[]{:S(2)}) collective-permute-start(bf16[416,256]{1,0:T(8,128)(2,1)S(1)} %pad_maximum_fusion.own), channel_id=1, source_target_pairs={{0,10},{1,7},{2,12},{3,9},{4,14},{5,11},{6,0},{7,13},{8,2},{9,15},... | collective-permute-start | bytes 638984 | tf_op jit(solution)/shard_map/ppermute | solution.py:158
  53.1 15.1 %collective-permute-start.9 = (bf16[416,256]{1,0:T(8,128)(2,1)S(1)}, bf16[416,256]{1,0:T(8,128)(2,1)S(1)}, u32[]{:S(2)}, u32[]{:S(2)}) collective-permute-start(bf16[416,256]{1,0:T(8,128)(2,1)S(1)} %pad_maximum_fusion.own), channel_id=1, source_target_pairs={{0,12},{1,5},{2,14},{3,7},{4,0},{5,9},{6,2},{7,11},{8,4},{9,13},{1... | collective-permute-start | bytes 638984 | tf_op jit(solution)/shard_map/ppermute | solution.py:158
  53.5 18.3 %collective-permute-start.8 = (bf16[416,256]{1,0:T(8,128)(2,1)S(1)}, bf16[416,256]{1,0:T(8,128)(2,1)S(1)}, u32[]{:S(2)}, u32[]{:S(2)}) collective-permute-start(bf16[416,256]{1,0:T(8,128)(2,1)S(1)} %pad_maximum_fusion.own), channel_id=1, source_target_pairs={{0,14},{1,3},{2,0},{3,5},{4,2},{5,7},{6,4},{7,9},{8,6},{9,11},{10,... | collective-permute-start | bytes 638984 | tf_op jit(solution)/shard_map/ppermute | solution.py:158
  53.8 18.0 %collective-permute-start.14 = (bf16[224,256]{1,0:T(8,128)(2,1)S(1)}, bf16[224,256]{1,0:T(8,128)(2,1)S(1)}, u32[]{:S(2)}, u32[]{:S(2)}) collective-permute-start(bf16[224,256]{1,0:T(8,128)(2,1)S(1)} %pad_maximum_fusion.2), channel_id=1, source_target_pairs={{0,8},{1,9},{2,10},{3,11},{4,12},{5,13},{6,14},{7,15},{8,0},{9,1},... | collective-permute-start | bytes 344072 | tf_op jit(solution)/shard_map/ppermute | solution.py:158
  61.7 15.5 %collective-permute-start.13 = (bf16[416,256]{1,0:T(8,128)(2,1)S(1)}, bf16[416,256]{1,0:T(8,128)(2,1)S(1)}, u32[]{:S(2)}, u32[]{:S(2)}) collective-permute-start(bf16[416,256]{1,0:T(8,128)(2,1)S(1)} %collective-permute-done.10.near3), channel_id=1, source_target_pairs={{0,1},{1,0},{2,3},{3,2},{4,5},{5,4},{6,7},{7,6},{8,9},{9,8},{10,11... | collective-permute-start | bytes 638984 | tf_op jit(solution)/shard_map/ppermute | solution.py:158
  68.1 9.2 %collective-permute-start.12 = (bf16[416,256]{1,0:T(8,128)(2,1)S(1)}, bf16[416,256]{1,0:T(8,128)(2,1)S(1)}, u32[]{:S(2)}, u32[]{:S(2)}) collective-permute-start(bf16[416,256]{1,0:T(8,128)(2,1)S(1)} %collective-permute-done.9.near2), channel_id=1, source_target_pairs={{0,1},{1,0},{2,3},{3,2},{4,5},{5,4},{6,7},{7,6},{8,9},{9,8},{10,11... | collective-permute-start | bytes 638984 | tf_op jit(solution)/shard_map/ppermute | solution.py:158
  71.8 5.5 %collective-permute-start.11 = (bf16[416,256]{1,0:T(8,128)(2,1)S(1)}, bf16[416,256]{1,0:T(8,128)(2,1)S(1)}, u32[]{:S(2)}, u32[]{:S(2)}) collective-permute-start(bf16[416,256]{1,0:T(8,128)(2,1)S(1)} %collective-permute-done.8.near1), channel_id=1, source_target_pairs={{0,1},{1,0},{2,3},{3,2},{4,5},{5,4},{6,7},{7,6},{8,9},{9,8},{10,11... | collective-permute-start | bytes 638984 | tf_op jit(solution)/shard_map/ppermute | solution.py:158
  71.8 5.5 %collective-permute-start.15 = (bf16[224,256]{1,0:T(8,128)(2,1)S(1)}, bf16[224,256]{1,0:T(8,128)(2,1)S(1)}, u32[]{:S(2)}, u32[]{:S(2)}) collective-permute-start(bf16[224,256]{1,0:T(8,128)(2,1)S(1)} %collective-permute-done.14.far), channel_id=1, source_target_pairs={{0,1},{1,0},{2,3},{3,2},{4,5},{5,4},{6,7},{7,6},{8,9},{9,8},{10,11... | collective-permute-start | bytes 344072 | tf_op jit(solution)/shard_map/ppermute | solution.py:158
  77.3 0.7 copy-start.1

commit v3 on v2

--- a/solution.py
+++ b/solution.py
@@ -12,8 +12,9 @@
 LINE = 8
 CUT = NB // LINE
 PIECE = SLOTS * CUT
-
-SMEM = pl.BlockSpec(memory_space=pltpu.SMEM)
+PARTS = 3
+STRIP = SLOTS * NB // PARTS
+
 VMEM = pl.BlockSpec(memory_space=pltpu.VMEM)
 HBM = pl.BlockSpec(memory_space=pltpu.HBM)
 ANY = pl.BlockSpec(memory_space=pl.ANY)
@@ -43,6 +44,19 @@
 
 
 TARGETS = targets()
+
+
+def packed(numbers):
+    word = sum(number << (4 * i) for i, number in enumerate(numbers))
+    return word - (1 << 32) if word >= 1 << 31 else word
+
+
+def target(q, rank):
+    low = packed([TARGETS[r][q] for r in range(SIDE // 2)])
+    high = packed([TARGETS[r][q] for r in range(SIDE // 2, SIDE)])
+    word = jnp.where(rank < SIDE // 2, jnp.int32(low), jnp.int32(high))
+    return jnp.bitwise_and(jnp.right_shift(word, 4 * lax.rem(rank, SIDE // 2)), 15)
+
 LEFT, RIGHT = pl.ds(0, NB), pl.ds(NB, NB)
 
 
@@ -66,7 +80,7 @@
     keep(f, RIGHT, rank, 2)
 
 
-def finish_kernel(order_ref, inv, own, near1, near2, near3, swap1, swap2, swap3, far, swap4, cols, matrix,
+def finish_kernel(inv, own, near1, near2, near3, swap1, swap2, swap3, far, swap4, cols, matrix,
                   factored, panels, held, edge, rows_x, cols_x, base, rows_f, cols_f, sem_m, sem_e, sem_o):
     row, col = lax.axis_index("row"), lax.axis_index("col")
     z, core = col // 2, lax.rem(col, 2)
@@ -74,8 +88,9 @@
     for c in edges:
         c.start()
     loads = []
-    for b in range(SLOTS):
-        loads.append(pltpu.make_async_copy(matrix.at[pl.ds(NB * b, NB)], held.at[b], sem_m.at[b]))
+    for b in range(PARTS):
+        at = pl.ds(STRIP * b, STRIP)
+        loads.append(pltpu.make_async_copy(matrix.at[at], held.at[at], sem_m.at[b]))
         loads[b].start()
 
     def place(msg, slot):
@@ -90,7 +105,7 @@
         place(swap, jnp.where(core == 0, down, up))
     for s in range(LINE):
         for h in range(2):
-            cols_x[h, :, s] = cols[order_ref[col * SIDE + 2 * s + h]].reshape(SLOTS, CUT, NB)
+            cols_x[h, :, s] = cols[target(2 * s + h, col)].reshape(SLOTS, CUT, NB)
     for c in edges:
         c.wait()
     across = lax.rem(z + LINE // 2, LINE)
@@ -99,15 +114,15 @@
     base[across] = edge[0, pl.ds(PIECE, CUT)]
     pivot = dot_t(base[...].reshape(NB, NB), inv[0]).astype(jnp.bfloat16)
     factor(rows_f, rows_x[0].reshape(SLOTS * NB, NB), rows_x[1].reshape(SLOTS * NB, NB), pivot, inv, row)
-    stores = [pltpu.make_async_copy(rows_f, panels, sem_o.at[SLOTS])]
+    stores = [pltpu.make_async_copy(rows_f, panels, sem_o.at[PARTS])]
     stores[0].start()
     factor(cols_f, cols_x[0].reshape(SLOTS * NB, NB), cols_x[1].reshape(SLOTS * NB, NB), pivot, inv, col)
-    for b in range(SLOTS):
+    for b in range(PARTS):
         loads[b].wait()
-        at = pl.ds(NB * b, NB)
-        value = held[b].astype(jnp.float32) - dot_t(rows_f[at, :], cols_f[...])
-        held[b] = value.astype(jnp.bfloat16)
-        stores.append(pltpu.make_async_copy(held.at[b], factored.at[at], sem_o.at[b]))
+        at = pl.ds(STRIP * b, STRIP)
+        value = held[at, :].astype(jnp.float32) - dot_t(rows_f[at, :], cols_f[...])
+        held[at, :] = value.astype(jnp.bfloat16)
+        stores.append(pltpu.make_async_copy(held.at[at], factored.at[at], sem_o.at[b]))
         stores[-1].start()
     for c in stores:
         c.wait()
@@ -122,25 +137,25 @@
             jax.ShapeDtypeStruct(matrix.shape, jnp.bfloat16),
             jax.ShapeDtypeStruct((rows, 2 * NB), jnp.bfloat16),
         ),
-        in_specs=[SMEM] + [VMEM] * 8 + [ANY, ANY, VMEM, HBM],
+        in_specs=[VMEM] * 8 + [ANY, ANY, VMEM, HBM],
         out_specs=(HBM, HBM),
         scratch_shapes=[
-            pltpu.VMEM((SLOTS, NB, columns), jnp.bfloat16),
+            pltpu.VMEM((rows, columns), jnp.bfloat16),
             pltpu.VMEM((2,) + far.shape, jnp.bfloat16),
             pltpu.VMEM((2, SLOTS, LINE, CUT, NB), jnp.bfloat16),
             pltpu.VMEM((2, SLOTS, LINE, CUT, NB), jnp.bfloat16),
             pltpu.VMEM((LINE, CUT, NB), jnp.bfloat16),
             pltpu.VMEM((rows, 2 * NB), jnp.bfloat16),
             pltpu.VMEM((columns, 2 * NB), jnp.bfloat16),
-            pltpu.SemaphoreType.DMA((SLOTS,)),
+            pltpu.SemaphoreType.DMA((PARTS,)),
             pltpu.SemaphoreType.DMA((2,)),
-            pltpu.SemaphoreType.DMA((SLOTS + 1,)),
+            pltpu.SemaphoreType.DMA((PARTS + 1,)),
         ],
         compiler_params=pltpu.CompilerParams(vmem_limit_bytes=36 * MIB),
         cost_estimate=pl.CostEstimate(
             flops=2 * rows * columns * 2 * NB, bytes_accessed=4 * rows * columns, transcendentals=0
         ),
-    )(jnp.asarray(TARGETS, jnp.int32).reshape(-1), inverses, own, *near, *swaps[:3], far, swaps[3], cols, matrix)
+    )(inverses, own, *near, *swaps[:3], far, swaps[3], cols, matrix)
 
 
 def moves(step):

time: 87.7 us -> 85.7 us (0.977)
  Pallas kernels: 8.62 us -> 7.53 us
    pallas_call x1, Pallas kernels: 8.62 us -> 7.53 us  [finish(): pl.pallas_call(finish_kernel, out_shape=(jax.ShapeDtypeStruct(matrix.shap...]
where the time goes in v3:
time: 85.7 us; the launch traced here: 84.8 us
  starting transfers between devices  48.8 us (57%)
  waiting for transfers between devices  24.3 us (28%)
  Pallas kernels  7.53 us (9%)
  local copies, waits for them, and re-layouts  3.27 us (4%)
    ppermute x17, starting transfers between devices, send(): return lax.ppermute(value, BOTH, pairs)  29.5 us
    ppermute x17, waiting for transfers between devices, send(): return lax.ppermute(value, BOTH, pairs)  24.3 us
    all_to_all x2, starting transfers between devices, shared(): lax.all_to_all(spread, axis, 0, 0, tiled=True, axis_index_groups=groups)  19.3 us
    pallas_call x1, Pallas kernels, finish(): pl.pallas_call(finish_kernel, out_shape=(jax.ShapeDtypeStruct(matrix.shap...  7.53 us
    broadcast_in_dim x3, local copies, waits for them, and re-layouts, shared(): jnp.broadcast_to(piece[None], (copies,) + piece.shape).reshape(-1, NB)  2.03 us
  transfers between devices with their start and end apart: 19, of which 7 were waited for; matrix products, arithmetic and copies ran while one was open for 0% of the time, Pallas kernels for 0%

profile of v3, /device:TPU:99, one launch (start us, length us, event | category | flops | bytes accessed | tf_op | source)
XLA Modules:
  0.0 84.8 jit_solution(13068338151522145995)
XLA Ops:
  0.6 1.2 %slice.45 = bf16[1536,256]{1,0:T(8,128)(2,1)S(1)} slice(bf16[1536,1536]{1,0:T(8,128)(2,1)} %matrix.1), slice={[0:1536], [0:256]} | slice | bytes 1572864 | tf_op jit(solution)/shard_map/slice | solution.py:190
  1.8 0.1 slice_bitcast_fusion.6
  1.9 0.7 collective-permute-start
  2.6 0.7 collective-permute-start.5
  3.2 1.3 %collective-permute-start.4 = (bf16[6,32,256]{2,1,0:T(8,128)(2,1)S(1)}, bf16[6,32,256]{2,1,0:T(8,128)(2,1)S(1)}, u32[]{:S(2)}, u32[]{:S(2)}) collective-permute-start(bf16[6,32,256]{2,1,0:T(8,128)(2,1)S(1)} %get-tuple-element.4), channel_id=1, source_target_pairs={{0,6},{1,7},{16,22},{17,23},{32,38},{33,39},{48,54},{49,55},{64,70... | collective-permute-start | bytes 294920 | tf_op jit(solution)/shard_map/ppermute | solution.py:173
  4.5 0.7 collective-permute-start.3
  5.2 0.7 collective-permute-start.2
  5.9 0.0 collective-permute-done
  5.9 0.7 collective-permute-start.1
  6.6 0.0 collective-permute-done.5
  6.6 0.7 collective-permute-start.6
  7.3 3.8 %collective-permute-done.4 = bf16[6,32,256]{2,1,0:T(8,128)(2,1)S(1)} collective-permute-done((bf16[6,32,256]{2,1,0:T(8,128)(2,1)S(1)}, bf16[6,32,256]{2,1,0:T(8,128)(2,1)S(1)}, u32[]{:S(2)}, u32[]{:S(2)}) %collective-permute-start.4) | collective-permute-done | bytes 98336 | tf_op jit(solution)/shard_map/ppermute | solution.py:173
  11.1 0.0 collective-permute-done.3
  11.1 0.0 collective-permute-done.2
  11.1 0.0 collective-permute-done.1
  11.1 0.0 collective-permute-done.6
  11.1 0.7 broadcast_in_dim.20
  11.9 6.9 %all-to-all-start = ((bf16[16,32,256]{2,1,0:T(8,128)(2,1)}), bf16[16,32,256]{2,1,0:T(8,128)(2,1)S(1)}, u32[]{:S(2)}, u32[]{:S(2)}) async-start(bf16[16,32,256]{2,1,0:T(8,128)(2,1)} %broadcast_in_dim.20), calls=%async_computation | async-start | bytes 524288 | tf_op jit(solution)/shard_map/all_to_all | solution.py:179
  18.8 7.3 %collective-permute-start.16 = (bf16[192,256]{1,0:T(8,128)(2,1)S(1)}, bf16[192,256]{1,0:T(8,128)(2,1)S(1)}, u32[]{:S(2)}, u32[]{:S(2)}) collective-permute-start(bf16[192,256]{1,0:T(8,128)(2,1)S(1)} %bitcast.76), channel_id=1, source_target_pairs={{0,224},{1,160},{2,240},{3,96},{4,80},{5,112},{6,48},{7,64},{8,0},... | collective-permute-start | bytes 294920 | tf_op jit(solution)/shard_map/ppermute | solution.py:173
  26.1 5.8 %collective-permute-done.16 = bf16[192,256]{1,0:T(8,128)(2,1)S(1)} collective-permute-done((bf16[192,256]{1,0:T(8,128)(2,1)S(1)}, bf16[192,256]{1,0:T(8,128)(2,1)S(1)}, u32[]{:S(2)}, u32[]{:S(2)}) %collective-permute-start.16) | collective-permute-done | bytes 98336 | tf_op jit(solution)/shard_map/ppermute | solution.py:173
  32.0 0.0 all-to-all-done
  32.0 1.3 %broadcast_in_dim.21 = bf16[16,192,256]{2,1,0:T(8,128)(2,1)} broadcast(bf16[192,256]{1,0:T(8,128)(2,1)S(1)} %collective-permute-done.16), dimensions={1,2} | broadcast | bytes 1671168 | tf_op jit(solution)/shard_map/broadcast_in_dim | solution.py:178
  33.3 0.0 copy-start
  33.3 12.4 %all-to-all-start.1 = ((bf16[16,192,256]{2,1,0:T(8,128)(2,1)}), bf16[16,192,256]{2,1,0:T(8,128)(2,1)S(1)}, u32[]{:S(2)}, u32[]{:S(2)}) async-start(bf16[16,192,256]{2,1,0:T(8,128)(2,1)} %broadcast_in_dim.21), calls=%async_computation.1 | async-start | bytes 3145728 | tf_op jit(solution)/shard_map/all_to_all | solution.py:179
  45.7 1.0 %collective-permute-start.7 = (bf16[224,256]{1,0:T(8,128)(2,1)S(1)}, bf16[224,256]{1,0:T(8,128)(2,1)S(1)}, u32[]{:S(2)}, u32[]{:S(2)}) collective-permute-start(bf16[224,256]{1,0:T(8,128)(2,1)S(1)} %pad_maximum_fusion.1), channel_id=1, source_target_pairs={{0,1},{1,0},{2,3},{3,2},{4,5},{5,4},{6,7},{7,6},{8,9},{9,8},{10,11... | collective-permute-start | bytes 344072 | tf_op jit(solution)/shard_map/ppermute | solution.py:173
  46.7 1.0 %collective-permute-done.7 = bf16[224,256]{1,0:T(8,128)(2,1)S(1)} collective-permute-done((bf16[224,256]{1,0:T(8,128)(2,1)S(1)}, bf16[224,256]{1,0:T(8,128)(2,1)S(1)}, u32[]{:S(2)}, u32[]{:S(2)}) %collective-permute-start.7) | collective-permute-done | bytes 114720 | tf_op jit(solution)/shard_map/ppermute | solution.py:173
  47.7 5.4 %collective-permute-start.10 = (bf16[416,256]{1,0:T(8,128)(2,1)S(1)}, bf16[416,256]{1,0:T(8,128)(2,1)S(1)}, u32[]{:S(2)}, u32[]{:S(2)}) collective-permute-start(bf16[416,256]{1,0:T(8,128)(2,1)S(1)} %pad_maximum_fusion.own), channel_id=1, source_target_pairs={{0,10},{1,7},{2,12},{3,9},{4,14},{5,11},{6,0},{7,13},{8,2},{9,15},... | collective-permute-start | bytes 638984 | tf_op jit(solution)/shard_map/ppermute | solution.py:173
  53.1 0.5 collective-permute-start.9
  53.5 0.3 collective-permute-start.8
  53.8 5.3 %collective-permute-start.14 = (bf16[224,256]{1,0:T(8,128)(2,1)S(1)}, bf16[224,256]{1,0:T(8,128)(2,1)S(1)}, u32[]{:S(2)}, u32[]{:S(2)}) collective-permute-start(bf16[224,256]{1,0:T(8,128)(2,1)S(1)} %pad_maximum_fusion.2), channel_id=1, source_target_pairs={{0,8},{1,9},{2,10},{3,11},{4,12},{5,13},{6,14},{7,15},{8,0},{9,1},... | collective-permute-start | bytes 344072 | tf_op jit(solution)/shard_map/ppermute | solution.py:173
  59.1 2.7 %collective-permute-done.10.near3 = bf16[416,256]{1,0:T(8,128)(2,1)S(1)} collective-permute-done((bf16[416,256]{1,0:T(8,128)(2,1)S(1)}, bf16[416,256]{1,0:T(8,128)(2,1)S(1)}, u32[]{:S(2)}, u32[]{:S(2)}) %collective-permute-start.10) | collective-permute-done | bytes 213024 | tf_op jit(solution)/shard_map/ppermute | solution.py:173
  61.7 0.0 collective-permute-start.13
  61.7 6.4 %collective-permute-done.9.near2 = bf16[416,256]{1,0:T(8,128)(2,1)S(1)} collective-permute-done((bf16[416,256]{1,0:T(8,128)(2,1)S(1)}, bf16[416,256]{1,0:T(8,128)(2,1)S(1)}, u32[]{:S(2)}, u32[]{:S(2)}) %collective-permute-start.9) | collective-permute-done | bytes 213024 | tf_op jit(solution)/shard_map/ppermute | solution.py:173
  68.1 0.0 collective-permute-start.12
  68.1 3.7 %collective-permute-done.8.near1 = bf16[416,256]{1,0:T(8,128)(2,1)S(1)} collective-permute-done((bf16[416,256]{1,0:T(8,128)(2,1)S(1)}, bf16[416,256]{1,0:T(8,128)(2,1)S(1)}, u32[]{:S(2)}, u32[]{:S(2)}) %collective-permute-start.8) | collective-permute-done | bytes 213024 | tf_op jit(solution)/shard_map/ppermute | solution.py:173
  71.8 0.0 collective-permute-start.11
  71.8 0.0 collective-permute-done.14.far
  71.8 4.5 %collective-permute-start.15 = (bf16[224,256]{1,0:T(8,128)(2,1)S(1)}, bf16[224,256]{1,0:T(8,128)(2,1)S(1)}, u32[]{:S(2)}, u32[]{:S(2)}) collective-permute-start(bf16[224,256]{1,0:T(8,128)(2,1)S(1)} %collective-permute-done.14.far), channel_id=1, source_target_pairs={{0,1},{1,0},{2,3},{3,2},{4,5},{5,4},{6,7},{7,6},{8,9},{9,8},{10,11... | collective-permute-start | bytes 344072 | tf_op jit(solution)/shard_map/ppermute | solution.py:173
  76.3 1.0 %collective-permute-done.15.swap4 = bf16[224,256]{1,0:T(8,128)(2,1)S(1)} collective-permute-done((bf16[224,256]{1,0:T(8,128)(2,1)S(1)}, bf16[224,256]{1,0:T(8,128)(2,1)S(1)}, u32[]{:S(2)}, u32[]{:S(2)}) %collective-permute-start.15) | collective-permute-done | bytes 114720 | tf_op jit(solution)/shard_map/ppermute | solution.py:173
  77.3 0.0 collective-permute-done.13.swap3
  77.3 0.0 collective-permute-done.12.swap2
  77.3 0.0 collective-permute-done.11.swap1
  77.3 0.0 all-to-all-done.1.cols
  77.3 0.0 copy-done
  77.3 7.5 %shard_map.41 = (bf16[1536,1536]{1,0:T(8,128)(2,1)}, bf16[1536,512]{1,0:T(8,128)(2,1)}) custom-call(bf16[2,256,256]{2,1,0:T(8,128)(2,1)S(1)} %copy-done, bf16[416,256]{1,0:T(8,128)(2,1)S(1)} %pad_maximum_fusion.own, bf16[416,256]{1,0:T(8,128)(2,1)S(1)} %collective-permute-done.8.near1, bf16[416,256]{1,0:T(8,128)(2,1)S(1)} %collective-permute-done.9.near2, ...), custom_call_target="tpu_custom_call" | custom-call | flops 2415919104 | bytes 9437184 | tf_op jit(solution)/shard_map/pallas_call | solution.py:134
  (8 shorter events, 0.1 us)
Async XLA Ops:
  1.9 4.0 %collective-permute-start = (bf16[6,32,256]{2,1,0:T(8,128)(2,1)S(1)}, bf16[6,32,256]{2,1,0:T(8,128)(2,1)S(1)}, u32[]{:S(2)}, u32[]{:S(2)}) collective-permute-start(bf16[6,32,256]{2,1,0:T(8,128)(2,1)S(1)} %get-tuple-element.2), channel_id=1, source_target_pairs={{0,2},{1,3},{16,18},{17,19},{32,34},{33,35},{48,50},{49,51},{64,66... | collective-permute-start | bytes 294920 | tf_op jit(solution)/shard_map/ppermute | solution.py:173
  2.6 4.0 %collective-permute-start.5 = (bf16[6,32,256]{2,1,0:T(8,128)(2,1)S(1)}, bf16[6,32,256]{2,1,0:T(8,128)(2,1)S(1)}, u32[]{:S(2)}, u32[]{:S(2)}) collective-permute-start(bf16[6,32,256]{2,1,0:T(8,128)(2,1)S(1)} %get-tuple-element.3), channel_id=1, source_target_pairs={{0,4},{1,5},{16,20},{17,21},{32,36},{33,37},{48,52},{49,53},{64,68... | collective-permute-start | bytes 294920 | tf_op jit(solution)/shard_map/ppermute | solution.py:173
  3.2 7.8 %collective-permute-start.4 = (bf16[6,32,256]{2,1,0:T(8,128)(2,1)S(1)}, bf16[6,32,256]{2,1,0:T(8,128)(2,1)S(1)}, u32[]{:S(2)}, u32[]{:S(2)}) collective-permute-start(bf16[6,32,256]{2,1,0:T(8,128)(2,1)S(1)} %get-tuple-element.4), channel_id=1, source_target_pairs={{0,6},{1,7},{16,22},{17,23},{32,38},{33,39},{48,54},{49,55},{64,70... | collective-permute-start | bytes 294920 | tf_op jit(solution)/shard_map/ppermute | solution.py:173
  4.5 6.5 %collective-permute-start.3 = (bf16[6,32,256]{2,1,0:T(8,128)(2,1)S(1)}, bf16[6,32,256]{2,1,0:T(8,128)(2,1)S(1)}, u32[]{:S(2)}, u32[]{:S(2)}) collective-permute-start(bf16[6,32,256]{2,1,0:T(8,128)(2,1)S(1)} %get-tuple-element.5), channel_id=1, source_target_pairs={{0,14},{1,15},{16,30},{17,31},{32,46},{33,47},{48,62},{49,63},{64,... | collective-permute-start | bytes 294920 | tf_op jit(solution)/shard_map/ppermute | solution.py:173
  5.2 5.9 %collective-permute-start.2 = (bf16[6,32,256]{2,1,0:T(8,128)(2,1)S(1)}, bf16[6,32,256]{2,1,0:T(8,128)(2,1)S(1)}, u32[]{:S(2)}, u32[]{:S(2)}) collective-permute-start(bf16[6,32,256]{2,1,0:T(8,128)(2,1)S(1)} %get-tuple-element.6), channel_id=1, source_target_pairs={{0,12},{1,13},{16,28},{17,29},{32,44},{33,45},{48,60},{49,61},{64,... | collective-permute-start | bytes 294920 | tf_op jit(solution)/shard_map/ppermute | solution.py:173
  5.9 5.2 %collective-permute-start.1 = (bf16[6,32,256]{2,1,0:T(8,128)(2,1)S(1)}, bf16[6,32,256]{2,1,0:T(8,128)(2,1)S(1)}, u32[]{:S(2)}, u32[]{:S(2)}) collective-permute-start(bf16[6,32,256]{2,1,0:T(8,128)(2,1)S(1)} %get-tuple-element.7), channel_id=1, source_target_pairs={{0,10},{1,11},{16,26},{17,27},{32,42},{33,43},{48,58},{49,59},{64,... | collective-permute-start | bytes 294920 | tf_op jit(solution)/shard_map/ppermute | solution.py:173
  6.6 4.5 %collective-permute-start.6 = (bf16[6,32,256]{2,1,0:T(8,128)(2,1)S(1)}, bf16[6,32,256]{2,1,0:T(8,128)(2,1)S(1)}, u32[]{:S(2)}, u32[]{:S(2)}) collective-permute-start(bf16[6,32,256]{2,1,0:T(8,128)(2,1)S(1)} %get-tuple-element.8), channel_id=1, source_target_pairs={{0,8},{1,9},{16,24},{17,25},{32,40},{33,41},{48,56},{49,57},{64,72... | collective-permute-start | bytes 294920 | tf_op jit(solution)/shard_map/ppermute | solution.py:173
  11.9 20.1 %all-to-all-start = ((bf16[16,32,256]{2,1,0:T(8,128)(2,1)}), bf16[16,32,256]{2,1,0:T(8,128)(2,1)S(1)}, u32[]{:S(2)}, u32[]{:S(2)}) async-start(bf16[16,32,256]{2,1,0:T(8,128)(2,1)} %broadcast_in_dim.20), calls=%async_computation | async-start | bytes 524288 | tf_op jit(solution)/shard_map/all_to_all | solution.py:179
  18.8 13.2 %collective-permute-start.16 = (bf16[192,256]{1,0:T(8,128)(2,1)S(1)}, bf16[192,256]{1,0:T(8,128)(2,1)S(1)}, u32[]{:S(2)}, u32[]{:S(2)}) collective-permute-start(bf16[192,256]{1,0:T(8,128)(2,1)S(1)} %bitcast.76), channel_id=1, source_target_pairs={{0,224},{1,160},{2,240},{3,96},{4,80},{5,112},{6,48},{7,64},{8,0},... | collective-permute-start | bytes 294920 | tf_op jit(solution)/shard_map/ppermute | solution.py:173
  33.3 44.0 %copy-start = (bf16[2,256,256]{2,1,0:T(8,128)(2,1)S(1)}, bf16[2,256,256]{2,1,0:T(8,128)(2,1)}, u32[]{:S(2)}) copy-start(bf16[2,256,256]{2,1,0:T(8,128)(2,1)} %inv.1) | copy-start | bytes 786436
  33.3 44.0 %all-to-all-start.1 = ((bf16[16,192,256]{2,1,0:T(8,128)(2,1)}), bf16[16,192,256]{2,1,0:T(8,128)(2,1)S(1)}, u32[]{:S(2)}, u32[]{:S(2)}) async-start(bf16[16,192,256]{2,1,0:T(8,128)(2,1)} %broadcast_in_dim.21), calls=%async_computation.1 | async-start | bytes 3145728 | tf_op jit(solution)/shard_map/all_to_all | solution.py:179
  45.7 2.0 %collective-permute-start.7 = (bf16[224,256]{1,0:T(8,128)(2,1)S(1)}, bf16[224,256]{1,0:T(8,128)(2,1)S(1)}, u32[]{:S(2)}, u32[]{:S(2)}) collective-permute-start(bf16[224,256]{1,0:T(8,128)(2,1)S(1)} %pad_maximum_fusion.1), channel_id=1, source_target_pairs={{0,1},{1,0},{2,3},{3,2},{4,5},{5,4},{6,7},{7,6},{8,9},{9,8},{10,11... | collective-permute-start | bytes 344072 | tf_op jit(solution)/shard_map/ppermute | solution.py:173
  47.7 14.1 %collective-permute-start.10 = (bf16[416,256]{1,0:T(8,128)(2,1)S(1)}, bf16[416,256]{1,0:T(8,128)(2,1)S(1)}, u32[]{:S(2)}, u32[]{:S(2)}) collective-permute-start(bf16[416,256]{1,0:T(8,128)(2,1)S(1)} %pad_maximum_fusion.own), channel_id=1, source_target_pairs={{0,10},{1,7},{2,12},{3,9},{4,14},{5,11},{6,0},{7,13},{8,2},{9,15},... | collective-permute-start | bytes 638984 | tf_op jit(solution)/shard_map/ppermute | solution.py:173
  53.1 15.1 %collective-permute-start.9 = (bf16[416,256]{1,0:T(8,128)(2,1)S(1)}, bf16[416,256]{1,0:T(8,128)(2,1)S(1)}, u32[]{:S(2)}, u32[]{:S(2)}) collective-permute-start(bf16[416,256]{1,0:T(8,128)(2,1)S(1)} %pad_maximum_fusion.own), channel_id=1, source_target_pairs={{0,12},{1,5},{2,14},{3,7},{4,0},{5,9},{6,2},{7,11},{8,4},{9,13},{1... | collective-permute-start | bytes 638984 | tf_op jit(solution)/shard_map/ppermute | solution.py:173
  53.5 18.3 %collective-permute-start.8 = (bf16[416,256]{1,0:T(8,128)(2,1)S(1)}, bf16[416,256]{1,0:T(8,128)(2,1)S(1)}, u32[]{:S(2)}, u32[]{:S(2)}) collective-permute-start(bf16[416,256]{1,0:T(8,128)(2,1)S(1)} %pad_maximum_fusion.own), channel_id=1, source_target_pairs={{0,14},{1,3},{2,0},{3,5},{4,2},{5,7},{6,4},{7,9},{8,6},{9,11},{10,... | collective-permute-start | bytes 638984 | tf_op jit(solution)/shard_map/ppermute | solution.py:173
  53.8 18.0 %collective-permute-start.14 = (bf16[224,256]{1,0:T(8,128)(2,1)S(1)}, bf16[224,256]{1,0:T(8,128)(2,1)S(1)}, u32[]{:S(2)}, u32[]{:S(2)}) collective-permute-start(bf16[224,256]{1,0:T(8,128)(2,1)S(1)} %pad_maximum_fusion.2), channel_id=1, source_target_pairs={{0,8},{1,9},{2,10},{3,11},{4,12},{5,13},{6,14},{7,15},{8,0},{9,1},... | collective-permute-start | bytes 344072 | tf_op jit(solution)/shard_map/ppermute | solution.py:173
  61.7 15.5 %collective-permute-start.13 = (bf16[416,256]{1,0:T(8,128)(2,1)S(1)}, bf16[416,256]{1,0:T(8,128)(2,1)S(1)}, u32[]{:S(2)}, u32[]{:S(2)}) collective-permute-start(bf16[416,256]{1,0:T(8,128)(2,1)S(1)} %collective-permute-done.10.near3), channel_id=1, source_target_pairs={{0,1},{1,0},{2,3},{3,2},{4,5},{5,4},{6,7},{7,6},{8,9},{9,8},{10,11... | collective-permute-start | bytes 638984 | tf_op jit(solution)/shard_map/ppermute | solution.py:173
  68.1 9.2 %collective-permute-start.12 = (bf16[416,256]{1,0:T(8,128)(2,1)S(1)}, bf16[416,256]{1,0:T(8,128)(2,1)S(1)}, u32[]{:S(2)}, u32[]{:S(2)}) collective-permute-start(bf16[416,256]{1,0:T(8,128)(2,1)S(1)} %collective-permute-done.9.near2), channel_id=1, source_target_pairs={{0,1},{1,0},{2,3},{3,2},{4,5},{5,4},{6,7},{7,6},{8,9},{9,8},{10,11... | collective-permute-start | bytes 638984 | tf_op jit(solution)/shard_map/ppermute | solution.py:173
  71.8 5.5 %collective-permute-start.11 = (bf16[416,256]{1,0:T(8,128)(2,1)S(1)}, bf16[416,256]{1,0:T(8,128)(2,1)S(1)}, u32[]{:S(2)}, u32[]{:S(2)}) collective-permute-start(bf16[416,256]{1,0:T(8,128)(2,1)S(1)} %collective-permute-done.8.near1), channel_id=1, source_target_pairs={{0,1},{1,0},{2,3},{3,2},{4,5},{5,4},{6,7},{7,6},{8,9},{9,8},{10,11... | collective-permute-start | bytes 638984 | tf_op jit(solution)/shard_map/ppermute | solution.py:173
  71.8 5.5 %collective-permute-start.15 = (bf16[224,256]{1,0:T(8,128)(2,1)S(1)}, bf16[224,256]{1,0:T(8,128)(2,1)S(1)}, u32[]{:S(2)}, u32[]{:S(2)}) collective-permute-start(bf16[224,256]{1,0:T(8,128)(2,1)S(1)} %collective-permute-done.14.far), channel_id=1, source_target_pairs={{0,1},{1,0},{2,3},{3,2},{4,5},{5,4},{6,7},{7,6},{8,9},{9,8},{10,11... | collective-permute-start | bytes 344072 | tf_op jit(solution)/shard_map/ppermute | solution.py:173
